TPU v7x, 256 devices: a whole 4x4x8 slice. The times are simulated.
256 devices in a mesh: section: 4 (over y), sample: 32 (over z, x), replica: 2 (over core).
Axes of the slice: x: 4, y: 4, z: 8, core: 2. Of those that a mesh axis runs over, the one named last changes fastest.
Arguments:
- saved_input: bfloat16 [4, 2, 64, 128, 512], P('section', None, ('sample', 'replica')), may hold values from -6 to 6
- out_grad: bfloat16 [2, 64, 128, 512], P(None, ('sample', 'replica')), may hold values from -4 to 4
- w_in: bfloat16 [4, 512, 2048], P('section'), may hold values from -0.25 to 0.25
- w_out: bfloat16 [4, 512, 512], P('section'), may hold values from -0.25 to 0.25
- item_owner: int32 [64, 2, 128, 1], P(('sample', 'replica')), may hold values from 0 to 127; in each aligned block of 64 rows (0 to 63, 64 to 127, ..., all dimensions but the last counted through in order) at most 2 rows name the same one
- item_slot: int32 [64, 2, 128], P(('sample', 'replica')), may hold values from 0 to 511
- table: float32 [65536, 512], P(('section', 'sample')), may hold values from -4 to 4
- moment: float32 [65536, 512], P(('section', 'sample')), may hold values from -3 to 3
- second: float32 [65536], P(('section', 'sample')), may hold values from 0.01 to 1
Outputs:
- grad_in: float32 [4, 512, 2048], P('section', 'sample')
- grad_out: float32 [4, 512, 512], P('section', 'sample')
- table_new: float32 [65536, 512], P(('section', 'sample'))
- moment_new: float32 [65536, 512], P(('section', 'sample'))
- second_new: float32 [65536], P(('section', 'sample'))
Inputs may be any that keep to these rules, and one draw needn't show every extreme that they name: `item_owner`: in each aligned block of 64 tokens, in the order sequence, micro-batch, position, no owner is named by more than 2 tokens.
All inputs are finite; a program needn't handle non-finite values.
Results may differ from a plain program's by a relative error of at most 0.029.
Values may be sent and summed in bfloat16 or wider, within the bound.
A program may use at most 128 MiB of HBM per device.

v0:
```python
import jax
import jax.numpy as jnp
from jax import lax
from jax.sharding import PartitionSpec as P

HEADS = 4
BLOCK = 64


LN_EPS = 1e-05
BETA_ONE = 0.8
BETA_TWO = 0.9
STEP_SIZE = 0.05
ADAM_EPS = 1e-08


def passed_along(value, axis, steps):
    count = lax.axis_size(axis)
    first, last = (max(0, -steps), min(count, count - steps))
    return lax.ppermute(value, axis, [(source, source + steps) for source in range(first, last)])


def contract(form, left, right):
    return jnp.einsum(form, left, right, preferred_element_type=jnp.float32)


def normalize(values):
    center = values - jnp.mean(values, -1, keepdims=True)
    inverse = lax.rsqrt(jnp.mean(center * center, -1, keepdims=True) + LN_EPS)
    return (center * inverse, inverse)


def norm_back(grad_norm, normed, inverse):
    return inverse * (
        grad_norm
        - jnp.mean(grad_norm, -1, keepdims=True)
        - normed * jnp.mean(grad_norm * normed, -1, keepdims=True)
    )


def silu_slope(values, sigmoid):
    return sigmoid * (1.0 + values * (1.0 - sigmoid))


def layer_back(layer_in, grad_top, weight_in, weight_out, head_count):
    batch, length, width = layer_in.shape
    head_size = width // head_count
    scale = head_size ** (-0.5)
    normed_in, inverse_in = normalize(layer_in.astype(jnp.float32))
    flat_in = normed_in.astype(jnp.bfloat16).reshape(batch * length, width)
    pre_act = jnp.dot(flat_in, weight_in, preferred_element_type=jnp.float32)
    pre_sig = jax.nn.sigmoid(pre_act)
    activ = lax.optimization_barrier((pre_act * pre_sig).astype(jnp.bfloat16))
    activ = activ.reshape(batch, length, 4, width)
    gates = activ[:, :, 0]
    values = activ[:, :, 1].reshape(batch, length, head_count, head_size)
    queries = activ[:, :, 2].reshape(batch, length, head_count, head_size)
    key_rows = activ[:, :, 3].reshape(batch, length, head_count, head_size)
    scores = contract("blhs,bmhs->bhlm", queries, key_rows) * scale
    causal = jnp.arange(length)[:, None] >= jnp.arange(length)[None, :]
    score_sig = jax.nn.sigmoid(scores)
    weights = jnp.where(causal, scores * score_sig, 0.0).astype(jnp.bfloat16)
    mixed = contract("bhlm,bmhs->blhs", weights, values).reshape(batch, length, width)
    normed_mix, inverse_mix = normalize(mixed)
    gate_vals = gates.astype(jnp.float32)
    hidden = (normed_mix * gate_vals).astype(jnp.bfloat16).reshape(batch * length, width)
    flat_top = grad_top.reshape(batch * length, width)
    grad_out = jnp.dot(hidden.T, flat_top, preferred_element_type=jnp.float32)
    grad_hidden = jnp.dot(flat_top, weight_out.T, preferred_element_type=jnp.float32).reshape(
        batch, length, width
    )
    grad_gate = grad_hidden * normed_mix
    grad_mix = norm_back(grad_hidden * gate_vals, normed_mix, inverse_mix).astype(jnp.bfloat16)
    grad_mix = grad_mix.reshape(batch, length, head_count, head_size)
    grad_weights = contract("blhs,bmhs->bhlm", grad_mix, values)
    grad_values = contract("bhlm,blhs->bmhs", weights, grad_mix)
    grad_scores = (
        jnp.where(causal, grad_weights * silu_slope(scores, score_sig), 0.0) * scale
    ).astype(jnp.bfloat16)
    grad_queries = contract("bhlm,bmhs->blhs", grad_scores, key_rows)
    grad_keys = contract("bhlm,blhs->bmhs", grad_scores, queries)
    slopes = silu_slope(pre_act, pre_sig).reshape(batch, length, 4, width)
    pieces = [
        grad_gate,
        grad_values.reshape(batch, length, width),
        grad_queries.reshape(batch, length, width),
        grad_keys.reshape(batch, length, width),
    ]
    grad_pre = jnp.concatenate(
        [(pieces[k] * slopes[:, :, k]).astype(jnp.bfloat16) for k in range(4)], -1
    )
    grad_pre = grad_pre.reshape(batch * length, 4 * width)
    grad_in = jnp.dot(flat_in.T, grad_pre, preferred_element_type=jnp.float32)
    grad_normed = jnp.dot(grad_pre, weight_in.T, preferred_element_type=jnp.float32).reshape(
        batch, length, width
    )
    grad_below = norm_back(grad_normed, normed_in, inverse_in) + grad_top.astype(jnp.float32)
    return (grad_below.astype(jnp.bfloat16), grad_in, grad_out)


def pack_rows(grad_blocks, owner_ids, slot_ids, live, owners_total, row_cap):
    count, rows_in = owner_ids.shape
    owner_hot = owner_ids[:, :, None] == jnp.arange(owners_total)[None, None, :]
    earlier = (jnp.arange(rows_in)[None, :] < jnp.arange(rows_in)[:, None]).astype(jnp.bfloat16)
    before = jnp.einsum(
        "tu,nuo->nto", earlier, owner_hot.astype(jnp.bfloat16), preferred_element_type=jnp.float32
    )
    rank = jnp.sum(jnp.where(owner_hot, before, 0.0), -1).astype(jnp.int32)
    placed = (
        owner_hot[..., None]
        & (rank[:, :, None, None] == jnp.arange(row_cap)[None, None, None, :])
        & live
    )
    sent = jnp.einsum(
        "ntoc,ntd->oncd",
        placed.astype(jnp.bfloat16),
        grad_blocks,
        preferred_element_type=jnp.float32,
    ).astype(jnp.bfloat16)
    sent_slots = jnp.sum(jnp.where(placed, slot_ids[:, :, None, None] + 1, 0), 1) - 1
    sent_slots = jnp.transpose(sent_slots, (1, 0, 2)).reshape(owners_total, count * row_cap)
    return (sent.reshape(owners_total, count * row_cap, grad_blocks.shape[-1]), sent_slots)


def local(saved_input, out_grad, w_in, w_out, item_owner, item_slot, table, moment, second):
    sections = lax.axis_size("section")
    position = lax.axis_index("section")
    micro = out_grad.shape[0]
    width = w_out.shape[2]
    layer_inputs = saved_input[0]
    acc_in = jnp.zeros(w_in.shape[1:], jnp.float32)
    acc_out = jnp.zeros(w_out.shape[1:], jnp.float32)
    incoming = jnp.zeros_like(out_grad[0])
    firsts = []
    for turn_num in range(sections + micro - 1):
        micro_idx = turn_num - (sections - 1 - position)
        active = (micro_idx >= 0) & (micro_idx < micro)
        picked = jnp.clip(micro_idx, 0, micro - 1)
        layer_in = lax.dynamic_index_in_dim(layer_inputs, picked, 0, keepdims=False)
        top_grad = lax.dynamic_index_in_dim(out_grad, picked, 0, keepdims=False)
        grad_top = jnp.where(position == sections - 1, top_grad, incoming)
        grad_top = jnp.where(active, grad_top, jnp.zeros_like(grad_top))
        grad_below, part_in, part_out = layer_back(layer_in, grad_top, w_in[0], w_out[0], HEADS)
        acc_in = acc_in + part_in
        acc_out = acc_out + part_out
        if turn_num >= sections - 1:
            firsts.append(grad_below)
        if turn_num < sections + micro - 2:
            incoming = passed_along(grad_below, "section", -1)
    factor = float(
        layer_inputs.shape[1]
        * layer_inputs.shape[2]
        * micro
        * lax.axis_size("sample")
        * lax.axis_size("replica")
    ) ** (-0.5)
    share_in, share_out = (
        lax.psum_scatter(
            acc_in.astype(jnp.bfloat16), "sample", scatter_dimension=0, tiled=True
        ).astype(jnp.float32),
        lax.psum_scatter(
            acc_out.astype(jnp.bfloat16), "sample", scatter_dimension=0, tiled=True
        ).astype(jnp.float32),
    )
    share_in, share_out = (
        lax.psum(share_in.astype(jnp.bfloat16), "replica").astype(jnp.float32),
        lax.psum(share_out.astype(jnp.bfloat16), "replica").astype(jnp.float32),
    )
    grad_in = (share_in * factor)[None]
    grad_out = (share_out * factor)[None]
    owners_total = sections * lax.axis_size("sample")
    row_cap = max(2, 2 * BLOCK // owners_total)
    token_grads = jnp.stack(firsts, 1).reshape(-1, width)
    blocks_total = token_grads.shape[0] // BLOCK
    owner_ids = item_owner.reshape(blocks_total, BLOCK)
    slot_ids = item_slot.reshape(blocks_total, BLOCK)
    grad_blocks = token_grads.reshape(blocks_total, BLOCK, width)
    live = position == 0
    sent, sent_slots = pack_rows(grad_blocks, owner_ids, slot_ids, live, owners_total, row_cap)
    taken, taken_slots = (
        lax.all_to_all(sent, ("section", "sample"), split_axis=0, concat_axis=0, tiled=True),
        lax.all_to_all(sent_slots, ("section", "sample"), split_axis=0, concat_axis=0, tiled=True),
    )
    flat_grads = taken.reshape(-1, width)
    flat_slots = taken_slots.reshape(-1)
    rows_own = table.shape[0]
    matches = flat_slots[None, :] == jnp.arange(rows_own)[:, None]
    row_grad = jnp.dot(matches.astype(jnp.bfloat16), flat_grads, preferred_element_type=jnp.float32)
    hits = jnp.sum(matches, 1).astype(jnp.float32)
    row_grad, hits = (
        lax.psum(row_grad.astype(jnp.bfloat16), "replica").astype(jnp.float32),
        lax.psum(hits.astype(jnp.bfloat16), "replica").astype(jnp.float32),
    )
    touched = hits > 0.5
    moment_new = jnp.where(
        touched[:, None], BETA_ONE * moment + (1.0 - BETA_ONE) * row_grad, moment
    )
    second_new = jnp.where(
        touched, BETA_TWO * second + (1.0 - BETA_TWO) * jnp.mean(row_grad * row_grad, -1), second
    )
    table_new = jnp.where(
        touched[:, None],
        table - STEP_SIZE * moment_new / (jnp.sqrt(second_new)[:, None] + ADAM_EPS),
        table,
    )
    return (grad_in, grad_out, table_new, moment_new, second_new)


def solution(mesh):
    placed = (
        P("section", None, ("sample", "replica"), None, None),
        P(None, ("sample", "replica"), None, None),
        P("section", None, None),
        P("section", None, None),
        P(("sample", "replica"), None, None, None),
        P(("sample", "replica"), None, None),
        P(("section", "sample"), None),
        P(("section", "sample"), None),
        P(("section", "sample")),
    )
    return jax.shard_map(
        local,
        mesh=mesh,
        in_specs=placed,
        out_specs=(
            P("section", "sample", None),
            P("section", "sample", None),
            P(("section", "sample"), None),
            P(("section", "sample"), None),
            P(("section", "sample")),
        ),
        check_vma=False,
    )
```

profile of v0, /device:TPU:1, one launch (start us, length us, event | category | flops | bytes accessed | tf_op | source)
XLA Modules:
  0.0 701.0 jit_solution(14980856303588807183)
XLA Ops:
  8.8 2.1 fusion.135
  11.0 2.6 add_multiply_fusion.4
  17.8 1.7 fusion.278
  20.6 2.5 copy.368
  23.1 2.1 fusion.324
  26.0 1.9 fusion.197
  27.9 1.9 fusion.234
  33.0 1.8 copy.498
  34.8 1.8 copy.473
  36.6 1.8 copy.499
  38.4 1.8 copy.474
  40.2 1.8 copy.500
  45.2 1.6 fusion.318
  47.7 1.6 collective-permute-start
  49.4 3.7 fusion.282
  53.1 1.9 add_multiply_fusion.3
  56.4 1.7 fusion.328
  64.3 2.9 reshape.2351
  67.2 4.9 fusion.323
  72.2 1.9 add_multiply_fusion.2
  75.5 1.7 fusion.327
  83.4 2.9 reshape.2363
  86.3 4.9 fusion.322
  91.3 1.9 add_multiply_fusion.1
  94.6 2.3 fusion.326
  103.1 2.9 reshape.2375
  106.0 4.9 fusion.321
  110.9 1.9 add_multiply_fusion
  114.3 1.7 fusion.325
  120.7 2.9 reshape.2387
  123.6 4.9 fusion.320
  136.1 1.8 copy.476
  137.9 1.8 copy.477
  139.7 1.8 copy.478
  144.7 1.9 fusion.317
  146.9 1.6 collective-permute-start.1
  148.5 2.8 fusion.281
  151.3 2.6 collective-permute-done.1
  158.4 1.8 copy.480
  160.2 1.8 copy.481
  162.0 1.8 copy.482
  167.0 1.9 fusion.316
  170.7 2.9 fusion.280
  173.5 1.5 collective-permute-done.2
  179.5 1.8 copy.484
  181.3 1.8 copy.485
  183.1 1.8 copy.486
  188.1 1.9 fusion.315
  191.7 2.8 fusion.279
  194.5 1.6 collective-permute-done.3
  204.2 8.4 %add_convert_fusion = bf16[512,2048]{1,0:T(8,128)(2,1)} fusion(f32[512,2048]{1,0:T(8,128)} %fusion.279, f32[512,2048]{1,0:T(8,128)} %fusion.280, f32[512,2048]{1,0:T(8,128)} %fusion.282, f32[512,2048]{1,0:T(8,128)} %fusion.281, bf16[1,128,512]{2,1,0:T(8,128)(2,1)S(1)} %fusion.147, bf16[1,128,512]{2,1,0:T(8,128)(2,1)S(1)} %fusion.149, ...), kind=kOutput, calls=%fused_computation | convolution fusion | flops 276037632 | bytes 19530756 | tf_op jit(solution)/shard_map/dot_general | solution.py:93
  216.1 16.6 %all-to-all-start = ((s32[128,1,8]{2,1,0:T(1,128)}), s32[128,1,8]{2,1,0:T(1,128)}, u32[]{:S(2)}, u32[]{:S(2)}) async-start(s32[128,1,8]{2,1,0:T(1,128)} %copy.453), calls=%async_computation.2 | async-start | bytes 131072 | tf_op jit(solution)/shard_map/all_to_all | solution.py:182
  235.2 1.8 copy.495
  237.8 2.0 fusion.314
  240.7 1.7 copy.454
  243.2 13.2 %all-to-all-start.1 = ((bf16[128,8,512]{2,1,0:T(8,128)(2,1)}), bf16[128,8,512]{2,1,0:T(8,128)(2,1)}, u32[]{:S(2)}, u32[]{:S(2)}) async-start(bf16[128,8,512]{2,1,0:T(8,128)(2,1)} %copy.454), calls=%async_computation.3 | async-start | bytes 2097152 | tf_op jit(solution)/shard_map/all_to_all | solution.py:181
  260.9 1.6 reduce.92
  262.6 18.5 %all-to-all-done.1 = bf16[128,8,512]{2,1,0:T(8,128)(2,1)} async-done(((bf16[128,8,512]{2,1,0:T(8,128)(2,1)}), bf16[128,8,512]{2,1,0:T(8,128)(2,1)}, u32[]{:S(2)}, u32[]{:S(2)}) %all-to-all-start.1) | async-done | bytes 1048608 | tf_op jit(solution)/shard_map/all_to_all | solution.py:181
  281.0 2.7 fusion.23
  283.8 150.5 %reduce-scatter.3.cloned.1.call-done = bf16[16,2048]{1,0:T(8,128)(2,1)} async-done(((bf16[512,2048]{1,0:T(8,128)(2,1)}), bf16[16,2048]{1,0:T(8,128)(2,1)}) %reduce-scatter.3.cloned.1.call-update) | async-done | bytes 65552 | tf_op jit(solution)/shard_map/reduce_scatter | solution.py:158
  434.6 215.8 %reduce-scatter.5.cloned.1.call-done = bf16[16,512]{1,0:T(8,128)(2,1)} async-done(((bf16[512,512]{1,0:T(8,128)(2,1)}), bf16[16,512]{1,0:T(8,128)(2,1)}) %reduce-scatter.5.cloned.1.call-update) | async-done | bytes 16400 | tf_op jit(solution)/shard_map/reduce_scatter | solution.py:161
  650.5 9.9 %all-reduce = (bf16[16,512]{1,0:T(8,128)(2,1)S(1)}, bf16[512]{0:T(512)(128)(2,1)S(1)}) all-reduce(bf16[16,512]{1,0:T(8,128)(2,1)} %reduce-scatter.5.cloned.1.call-done, bf16[512]{0:T(512)(128)(2,1)S(1)} %convert_convert_fusion), channel_id=1, replica_groups=mesh['section'=4,'sample'=32,'replica'=2] {'replica'}, use_global_device_ids=true, to_apply=%region_41.42 | all-reduce | flops 8704 | bytes 34816 | tf_op jit(solution)/shard_map/psum | solution.py:167
  661.0 26.9 %all-reduce.4.cloned.1.call-done = (bf16[16,2048]{1,0:T(8,128)(2,1)}, bf16[512,512]{1,0:T(8,128)(2,1)}) async-done(((bf16[16,2048]{1,0:T(8,128)(2,1)}, bf16[512,512]{1,0:T(8,128)(2,1)}), (bf16[16,2048]{1,0:T(8,128)(2,1)}, bf16[512,512]{1,0:T(8,128)(2,1)})) %all-reduce.4.cloned.1.call-update) | async-done | bytes 589840 | tf_op jit(solution)/shard_map/psum | solution.py:166
  691.2 3.0 subtract_select_fusion
  (493 shorter events, 97.1 us)
Async XLA Ops:
  7.2 427.1 %reduce-scatter.3.cloned.1.call-start = ((), (), s32[]{:S(2)}) async-start(), calls=%async_computation.4 | async-start | bytes 2162688 | tf_op jit(solution)/shard_map/reduce_scatter | solution.py:158
  8.8 4.8 copy-start.137
  8.8 4.8 copy-start.123
  8.8 4.8 copy-start.126
  8.8 4.8 copy-start.116
  8.8 4.8 copy-start.120
  16.8 6.3 copy-start.6
  17.6 8.4 %copy-start.21 = (bf16[1,128,1,512]{3,1,2,0:T(8,128)(2,1)}, bf16[1,128,1,512]{3,1,2,0:T(8,128)(2,1)S(1)}, u32[]{:S(2)}) copy-start(bf16[1,128,1,512]{3,1,2,0:T(8,128)(2,1)S(1)} %copy.497) | copy-start | bytes 393220
  34.8 10.4 %copy-start.1 = (bf16[1,2,1,128,512]{4,3,2,1,0:T(8,128)(2,1)S(1)}, bf16[1,2,1,128,512]{4,3,2,1,0:T(8,128)(2,1)}, u32[]{:S(2)}) copy-start(bf16[1,2,1,128,512]{4,3,2,1,0:T(8,128)(2,1)} %param.9) | copy-start | bytes 786436
  34.8 10.4 %copy-start.74 = (bf16[1,128,512]{2,1,0:T(8,128)(2,1)S(1)}, bf16[1,128,512]{2,1,0:T(8,128)(2,1)}, u32[]{:S(2)}) copy-start(bf16[1,128,512]{2,1,0:T(8,128)(2,1)} %get-tuple-element.86) | copy-start | bytes 393220
  47.7 81.4 %collective-permute-start = (bf16[1,128,512]{2,1,0:T(8,128)(2,1)}, bf16[1,128,512]{2,1,0:T(8,128)(2,1)}, u32[]{:S(2)}, u32[]{:S(2)}) collective-permute-start(bf16[1,128,512]{2,1,0:T(8,128)(2,1)} %fusion.207), channel_id=1, source_target_pairs={{64,0},{128,64},{192,128},{65,1},{129,65},{193,129},{66,2},{130,66... | collective-permute-start | bytes 393224 | tf_op jit(solution)/shard_map/ppermute | solution.py:20
  61.6 5.6 copy-start.99
  62.8 9.3 %copy-start.8 = (f32[4,128,128]{2,1,0:T(8,128)}, f32[4,128,128]{2,1,0:T(8,128)S(1)}, u32[]{:S(2)}) copy-start(f32[4,128,128]{2,1,0:T(8,128)S(1)} %get-tuple-element.113) | copy-start | bytes 786436
  62.8 9.3 %copy-start.103 = (f32[128]{0:T(128)}, f32[128]{0:T(128)S(1)}, u32[]{:S(2)}) copy-start(f32[128]{0:T(128)S(1)} %broadcast_multiply_fusion.22) | copy-start | bytes 1540
  64.3 7.8 %copy-start.155 = (f32[128]{0:T(128)S(1)}, f32[128]{0:T(128)}, u32[]{:S(2)}) copy-start(f32[128]{0:T(128)} %get-tuple-element.22) | copy-start | bytes 1540
  64.3 7.9 %copy-start.124 = (f32[128]{0:T(128)S(1)}, f32[128]{0:T(128)}, u32[]{:S(2)}) copy-start(f32[128]{0:T(128)} %copy-done.123) | copy-start | bytes 1540
  80.7 5.7 copy-start.97
  81.9 9.4 %copy-start.10 = (f32[4,128,128]{2,1,0:T(8,128)}, f32[4,128,128]{2,1,0:T(8,128)S(1)}, u32[]{:S(2)}) copy-start(f32[4,128,128]{2,1,0:T(8,128)S(1)} %get-tuple-element.116) | copy-start | bytes 786436
  81.9 9.4 %copy-start.105 = (f32[128]{0:T(128)}, f32[128]{0:T(128)S(1)}, u32[]{:S(2)}) copy-start(f32[128]{0:T(128)S(1)} %broadcast_multiply_fusion.16) | copy-start | bytes 1540
  83.4 7.9 %copy-start.154 = (f32[128]{0:T(128)S(1)}, f32[128]{0:T(128)}, u32[]{:S(2)}) copy-start(f32[128]{0:T(128)} %get-tuple-element.23) | copy-start | bytes 1540
  83.4 7.9 %copy-start.121 = (f32[128]{0:T(128)S(1)}, f32[128]{0:T(128)}, u32[]{:S(2)}) copy-start(f32[128]{0:T(128)} %copy-done.120) | copy-start | bytes 1540
  100.3 5.7 copy-start.95
  101.6 9.3 %copy-start.12 = (f32[4,128,128]{2,1,0:T(8,128)}, f32[4,128,128]{2,1,0:T(8,128)S(1)}, u32[]{:S(2)}) copy-start(f32[4,128,128]{2,1,0:T(8,128)S(1)} %get-tuple-element.119) | copy-start | bytes 786436
  101.6 9.3 %copy-start.108 = (f32[128]{0:T(128)}, f32[128]{0:T(128)S(1)}, u32[]{:S(2)}) copy-start(f32[128]{0:T(128)S(1)} %broadcast_multiply_fusion.10) | copy-start | bytes 1540
  103.1 7.8 %copy-start.153 = (f32[128]{0:T(128)S(1)}, f32[128]{0:T(128)}, u32[]{:S(2)}) copy-start(f32[128]{0:T(128)} %get-tuple-element.19) | copy-start | bytes 1540
  103.1 7.8 %copy-start.117 = (f32[128]{0:T(128)S(1)}, f32[128]{0:T(128)}, u32[]{:S(2)}) copy-start(f32[128]{0:T(128)} %copy-done.116) | copy-start | bytes 1540
  120.7 8.4 %copy-start.4 = (bf16[2,1,128,512]{3,2,1,0:T(8,128)(2,1)S(1)}, bf16[2,1,128,512]{3,2,1,0:T(8,128)(2,1)}, u32[]{:S(2)}) copy-start(bf16[2,1,128,512]{3,2,1,0:T(8,128)(2,1)} %param.10) | copy-start | bytes 786436
  128.6 4.6 copy-start.90
  146.8 7.5 %copy-start.16 = (f32[128,512]{1,0:T(8,128)S(1)}, f32[128,512]{1,0:T(8,128)}, u32[]{:S(2)}) copy-start(f32[128,512]{1,0:T(8,128)} %copy.479) | copy-start | bytes 786436
  146.9 7.5 %copy-start.64 = (bf16[1,128,1,512]{3,2,1,0:T(2,128)(2,1)S(1)}, bf16[1,128,1,512]{3,2,1,0:T(2,128)(2,1)}, u32[]{:S(2)}) copy-start(bf16[1,128,1,512]{3,2,1,0:T(2,128)(2,1)} %get-tuple-element.96) | copy-start | bytes 393220
  146.9 7.5 %copy-start.106 = (f32[128]{0:T(128)S(1)}, f32[128]{0:T(128)}, u32[]{:S(2)}) copy-start(f32[128]{0:T(128)} %copy-done.105) | copy-start | bytes 1540
  146.9 7.5 %copy-start.130 = (f32[128]{0:T(128)S(1)}, f32[128]{0:T(128)}, u32[]{:S(2)}) copy-start(f32[128]{0:T(128)} %add_rsqrt_fusion.4) | copy-start | bytes 1540
  146.9 7.1 %collective-permute-start.1 = (bf16[1,128,512]{2,1,0:T(8,128)(2,1)S(1)}, bf16[1,128,512]{2,1,0:T(8,128)(2,1)S(1)}, u32[]{:S(2)}, u32[]{:S(2)}) collective-permute-start(bf16[1,128,512]{2,1,0:T(8,128)(2,1)S(1)} %fusion.97), channel_id=1, source_target_pairs={{64,0},{128,64},{192,128},{65,1},{129,65},{193,129},{66,2},{130,66... | collective-permute-start | bytes 393224 | tf_op jit(solution)/shard_map/ppermute | solution.py:20
  169.2 6.2 copy-start.15
  169.2 6.2 copy-start.63
  169.2 6.2 copy-start.109
  169.2 6.2 copy-start.132
  169.2 5.8 collective-permute-start.2
  190.2 6.2 copy-start.62
  190.2 6.2 copy-start.112
  190.3 6.2 copy-start.134
  190.3 5.8 collective-permute-start.3
  198.9 5.3 copy-start.118
  199.0 5.3 copy-start.141
  201.5 11.1 %copy-start.70 = (bf16[1,128,512]{2,1,0:T(8,128)(2,1)}, bf16[1,128,512]{2,1,0:T(8,128)(2,1)S(1)}, u32[]{:S(2)}) copy-start(bf16[1,128,512]{2,1,0:T(8,128)(2,1)S(1)} %fusion.151) | copy-start | bytes 393220
  202.5 10.1 %copy-start.72 = (bf16[1,128,512]{2,1,0:T(8,128)(2,1)}, bf16[1,128,512]{2,1,0:T(8,128)(2,1)S(1)}, u32[]{:S(2)}) copy-start(bf16[1,128,512]{2,1,0:T(8,128)(2,1)S(1)} %fusion.149) | copy-start | bytes 393220
  212.6 20.0 %copy-start.7 = (f32[4,128,128]{2,1,0:T(8,128)S(1)}, f32[4,128,128]{2,1,0:T(8,128)}, u32[]{:S(2)}) copy-start(f32[4,128,128]{2,1,0:T(8,128)} %copy-done.6) | copy-start | bytes 786436
  212.7 20.8 %copy-start.9 = (f32[4,128,128]{2,1,0:T(8,128)S(1)}, f32[4,128,128]{2,1,0:T(8,128)}, u32[]{:S(2)}) copy-start(f32[4,128,128]{2,1,0:T(8,128)} %copy-done.8) | copy-start | bytes 786436
  212.7 21.7 %copy-start.13 = (f32[4,128,128]{2,1,0:T(8,128)S(1)}, f32[4,128,128]{2,1,0:T(8,128)}, u32[]{:S(2)}) copy-start(f32[4,128,128]{2,1,0:T(8,128)} %copy-done.12) | copy-start | bytes 786436
  212.7 24.3 %copy-start.11 = (f32[4,128,128]{2,1,0:T(8,128)S(1)}, f32[4,128,128]{2,1,0:T(8,128)}, u32[]{:S(2)}) copy-start(f32[4,128,128]{2,1,0:T(8,128)} %copy-done.10) | copy-start | bytes 786436
  216.1 27.1 %all-to-all-start = ((s32[128,1,8]{2,1,0:T(1,128)}), s32[128,1,8]{2,1,0:T(1,128)}, u32[]{:S(2)}, u32[]{:S(2)}) async-start(s32[128,1,8]{2,1,0:T(1,128)} %copy.453), calls=%async_computation.2 | async-start | bytes 131072 | tf_op jit(solution)/shard_map/all_to_all | solution.py:182
  240.6 15.9 %copy-start.5 = (bf16[2,1,128,512]{3,2,1,0:T(8,128)(2,1)S(1)}, bf16[2,1,128,512]{3,2,1,0:T(8,128)(2,1)}, u32[]{:S(2)}) copy-start(bf16[2,1,128,512]{3,2,1,0:T(8,128)(2,1)} %param.10) | copy-start | bytes 786436
  240.6 15.9 %copy-start.115 = (f32[128]{0:T(128)S(1)}, f32[128]{0:T(128)}, u32[]{:S(2)}) copy-start(f32[128]{0:T(128)} %copy-done.114) | copy-start | bytes 1540
  240.6 15.9 %copy-start.136 = (f32[128]{0:T(128)S(1)}, f32[128]{0:T(128)}, u32[]{:S(2)}) copy-start(f32[128]{0:T(128)} %add_rsqrt_fusion.8) | copy-start | bytes 1540
  242.3 14.2 %copy-start.22 = (bf16[1,128,1,512]{3,1,2,0:T(8,128)(2,1)S(1)}, bf16[1,128,1,512]{3,1,2,0:T(8,128)(2,1)}, u32[]{:S(2)}) copy-start(bf16[1,128,1,512]{3,1,2,0:T(8,128)(2,1)} %copy-done.21) | copy-start | bytes 393220
  242.3 15.6 %copy-start.30 = (bf16[1,128,1,512]{3,1,2,0:T(8,128)(2,1)S(1)}, bf16[1,128,1,512]{3,1,2,0:T(8,128)(2,1)}, u32[]{:S(2)}) copy-start(bf16[1,128,1,512]{3,1,2,0:T(8,128)(2,1)} %copy-done.29) | copy-start | bytes 393220
  242.3 15.6 %copy-start.58 = (f32[1,128,1,512]{3,1,2,0:T(8,128)S(1)}, f32[1,128,1,512]{3,1,2,0:T(8,128)}, u32[]{:S(2)}) copy-start(f32[1,128,1,512]{3,1,2,0:T(8,128)} %copy.492) | copy-start | bytes 786436
  242.3 15.6 %copy-start.104 = (f32[128]{0:T(128)S(1)}, f32[128]{0:T(128)}, u32[]{:S(2)}) copy-start(f32[128]{0:T(128)} %copy-done.103) | copy-start | bytes 1540
  242.3 15.6 %copy-start.129 = (f32[128]{0:T(128)S(1)}, f32[128]{0:T(128)}, u32[]{:S(2)}) copy-start(f32[128]{0:T(128)} %add_rsqrt_fusion.6) | copy-start | bytes 1540
  243.2 37.9 %all-to-all-start.1 = ((bf16[128,8,512]{2,1,0:T(8,128)(2,1)}), bf16[128,8,512]{2,1,0:T(8,128)(2,1)}, u32[]{:S(2)}, u32[]{:S(2)}) async-start(bf16[128,8,512]{2,1,0:T(8,128)(2,1)} %copy.454), calls=%async_computation.3 | async-start | bytes 2097152 | tf_op jit(solution)/shard_map/all_to_all | solution.py:181
  256.4 394.0 %reduce-scatter.5.cloned.1.call-start = ((), (), s32[]{:S(2)}) async-start(), calls=%async_computation.5 | async-start | bytes 540672 | tf_op jit(solution)/shard_map/reduce_scatter | solution.py:161
  260.8 427.1 %all-reduce.4.cloned.1.call-start = ((), (), s32[]{:S(2)}) async-start(), calls=%async_computation.6 | async-start | bytes 1179648 | tf_op jit(solution)/shard_map/psum | solution.py:166
  262.5 428.1 %copy-start.139 = (f32[512]{0:T(512)S(1)}, f32[512]{0:T(512)}, u32[]{:S(2)}) copy-start(f32[512]{0:T(512)} %param.17) | copy-start | bytes 6148
  262.6 428.6 %copy-start.61 = (f32[512,512]{1,0:T(8,128)S(1)}, f32[512,512]{1,0:T(8,128)}, u32[]{:S(2)}) copy-start(f32[512,512]{1,0:T(8,128)} %param.15) | copy-start | bytes 3145732
  (102 other events, 217.4 us)
Sparse Core Ops, SparseCore 0:
  212.8 221.4 reduce-scatter.2
  439.2 211.2 reduce-scatter.4
  653.7 34.1 all-reduce.3
where the time goes:
time: 708 us; the launch traced here: 701 us
  waiting for transfers between devices  418 us (59%)
  local copies, waits for them, and re-layouts  110 us (16%)
  matrix products  67.1 us (9%)
  other arithmetic  43.7 us (6%)
  starting transfers between devices  35.9 us (5%)
  between operations  16.4 us (2%)
  blocking collectives  9.92 us (1%)
    reduce_scatter x1, waiting for transfers between devices, local(): lax.psum_scatter(acc_out.astype(jnp.bfloat16), 'sample', scatter_dimensio...  216 us
    reduce_scatter x1, waiting for transfers between devices, local(): lax.psum_scatter(acc_in.astype(jnp.bfloat16), 'sample', scatter_dimension...  151 us
    psum x1, waiting for transfers between devices, local(): lax.psum(share_in.astype(jnp.bfloat16), 'replica').astype(jnp.float32)  26.9 us
    slice x5, local copies, waits for them, and re-layouts, layer_back(): slopes[:, :, k]  21.8 us
    convert_element_type x20, other arithmetic, layer_back(): (pieces[k] * slopes[:, :, k]).astype(jnp.bfloat16)  21.7 us
    unnamed x328, local copies, waits for them, and re-layouts  20.9 us
    dot_general x5, matrix products, layer_back(): grad_in = jnp.dot(flat_in.T, grad_pre, preferred_element_type=jnp.float32)  20.6 us
    all_to_all x1, waiting for transfers between devices, local(): lax.all_to_all(sent, ('section', 'sample'), split_axis=0, concat_axis=0,...  18.5 us
  transfers between devices with their start and end apart: 9, of which 8 were waited for; matrix products, arithmetic and copies ran while one was open for 15% of the time, Pallas kernels for 0%

commit v1 on v0

v1 whole, which is shorter than its diff:
```python
import functools

import jax
import jax.numpy as jnp
from jax import lax
from jax.experimental import pallas as pl
from jax.experimental.pallas import tpu as pltpu
from jax.sharding import PartitionSpec as P

HEADS = 4
BLOCK = 64
LN_EPS = 1e-05
BETA_ONE = 0.8
BETA_TWO = 0.9
STEP_SIZE = 0.05
ADAM_EPS = 1e-08

F32 = jnp.float32
BF = jnp.bfloat16
MESH = pl.DeviceIdType.MESH
PARTS = 5
LANES = 128


def mm(a, b):
    return jnp.dot(a, b, preferred_element_type=F32)


def mm_nt(a, b):
    return lax.dot_general(a, b, (((1,), (1,)), ((), ())), preferred_element_type=F32)


def sigmoid(v):
    return 0.5 + 0.5 * jnp.tanh(0.5 * v)


def mean(v):
    return jnp.mean(v, -1, keepdims=True)


def normed(v):
    center = v - mean(v)
    inverse = lax.rsqrt(mean(center * center) + LN_EPS)
    return center * inverse, inverse


def norm_back(grad, norm, inverse):
    return inverse * (grad - mean(grad) - norm * mean(grad * norm))


def slope(v, s):
    return s * (1.0 + v * (1.0 - s))


def kernel(
    dims,
    x_ref, og_ref, win_ref, wout_ref, owner_ref, slot_ref,
    rg_ref, hits_ref, gi_ref, go_ref,
    xn_s, rx_s, act_s, slope_s, w_s, zs_s, mn_s, rm_s,
    hx_s, hx_o, lt_s, g_s, below_s, d_s, d_r,
    gw_s, gx_r, gz_s, gz_r, f_s,
    p_s, tk_s, idp_s, idx_r, idz_s, idt_s, tp_s, tx_r, tz_s, tt_s, oh_s,
    hop_ss, hop_rs, hx_ss, hx_rs, d_ss, d_rs, gx_ss, gx_rs, gz_ss, gz_rs, f_ss, f_rs,
    tk_ss, tk_rs, ix_ss, ix_rs, iz_ss, iz_rs, ic_ss, ic_rs,
):
    ns, nz, nx, cap = dims
    micro, length, width = x_ref.shape
    half = width // 2
    hs = width // HEADS
    scale = hs ** (-0.5)
    rows = width // (nz * nx)
    own_rows = rg_ref.shape[0]
    piece = length // (nz * nx)
    sec = lax.axis_index("section")
    smp = lax.axis_index("sample")
    core = lax.axis_index("replica")
    zz, xx = lax.div(smp, nx), lax.rem(smp, nx)

    def wrap(v, n):
        return lax.rem(v, n)

    def x_peer(d):
        return (sec, zz * nx + wrap(xx + d, nx), core)

    def z_peer(d):
        return (sec, wrap(zz + d, nz) * nx + xx, core)

    other = (sec, smp, 1 - core)

    def remote(src, dst, ss, rs, dev):
        return pltpu.make_async_remote_copy(
            src_ref=src, dst_ref=dst, send_sem=ss, recv_sem=rs, device_id=dev, device_id_type=MESH
        )

    barrier = pltpu.get_barrier_semaphore()
    peers = [other]
    peers += [(wrap(sec + d, ns), smp, core) for d in range(1, ns)]
    peers += [x_peer(d) for d in range(1, nx)]
    peers += [z_peer(d) for d in range(1, nz)]
    for peer in peers:
        pl.semaphore_signal(barrier, inc=1, device_id=peer, device_id_type=MESH)

    row_id = lax.broadcasted_iota(jnp.int32, (length, length), 0)
    col_id = lax.broadcasted_iota(jnp.int32, (length, length), 1)

    def forward(m):
        xn, rx = normed(x_ref[m].astype(F32))
        xn_s[m] = xn
        rx_s[m] = rx
        xb = xn.astype(BF)
        hx_s[1, m] = xb
        for k in range(4):
            pre = mm(xb, win_ref[:, k * width:(k + 1) * width])
            s = sigmoid(pre)
            act_s[m, k] = (pre * s).astype(BF)
            slope_s[m, k] = slope(pre, s)
        causal = row_id >= col_id
        mixed = []
        for h in range(HEADS):
            cols = slice(h * hs, (h + 1) * hs)
            z = mm_nt(act_s[m, 2, :, cols], act_s[m, 3, :, cols]) * scale
            s = sigmoid(z)
            wt = jnp.where(causal, z * s, 0.0).astype(BF)
            w_s[m, h] = wt.T
            zs_s[m, h] = jnp.where(causal, slope(z, s), 0.0) * scale
            mixed.append(mm(wt, act_s[m, 1, :, cols]))
        mn, rm = normed(jnp.concatenate(mixed, -1))
        mn_s[m] = mn
        rm_s[m] = rm
        hx_s[0, m] = (mn * act_s[m, 0].astype(F32)).astype(BF)

    def keep(m, k, value):
        d_s[0, k, m] = value[:, :half]
        d_s[1, k, m] = value[:, half:]
        remote(d_s.at[1 - core, k, m], d_r.at[k, m], d_ss.at[k, m], d_rs.at[k, m], other).start()

    def backward(m):
        g = g_s[m]
        keep(m, 0, g)
        dh = mm_nt(g, wout_ref[...])
        mn = mn_s[m]
        dpre = [(dh * mn * slope_s[m, 0]).astype(BF)]
        keep(m, 1, dpre[0])
        dmix = norm_back(dh * act_s[m, 0].astype(F32), mn, rm_s[m]).astype(BF)
        dv, dq, dk = [], [], []
        for h in range(HEADS):
            cols = slice(h * hs, (h + 1) * hs)
            dm = dmix[:, cols]
            dw = mm_nt(dm, act_s[m, 1, :, cols])
            dv.append(mm(w_s[m, h], dm))
            dz = (dw * zs_s[m, h]).astype(BF)
            dq.append(mm(dz, act_s[m, 3, :, cols]))
            dk.append(mm(dz.T, act_s[m, 2, :, cols]))
        for k, part in enumerate((dv, dq, dk)):
            dpre.append((jnp.concatenate(part, -1) * slope_s[m, k + 1]).astype(BF))
            keep(m, k + 2, dpre[-1])
        dxn = mm_nt(dpre[0], win_ref[:, :width])
        for k in range(1, 4):
            dxn = dxn + mm_nt(dpre[k], win_ref[:, k * width:(k + 1) * width])
        below = norm_back(dxn, xn_s[m], rx_s[m]) + g.astype(F32)
        below_s[m] = below.astype(BF)

    def pack_plan(m):
        owner = owner_ref[m:m + 1, :]
        spread = jnp.broadcast_to(owner.astype(F32), (length, length))
        same = (spread == spread.T) & (lax.div(row_id, BLOCK) == lax.div(col_id, BLOCK)) & (row_id < col_id)
        rank = jnp.sum(jnp.where(same, 1.0, 0.0), 0, keepdims=True).astype(jnp.int32)
        place = owner - sec * (nz * nx)
        mine = (place >= 0) & (place < nz * nx)
        place = jnp.where(mine, place, 0)
        block = lax.div(lax.broadcasted_iota(jnp.int32, (1, length), 1), BLOCK)
        to = (lax.rem(place, nx) * nz + lax.div(place, nx)) * piece + block * cap + rank
        to = jnp.where(mine, to, -1)
        plan = jnp.where(row_id == to, 1.0, 0.0).astype(BF)
        p_s[m] = plan
        name = slot_ref[m:m + 1, :] + 1
        high, low = lax.div(name, 32), lax.rem(name, 32)
        both = jnp.where(row_id < length // 2, high, low).astype(F32).astype(BF)
        return mm_nt(plan, both).astype(BF)

    def x_start(pack, inbox, ss, rs):
        inbox[0] = pack[xx]
        for d in range(1, nx):
            remote(pack.at[wrap(xx + d, nx)], inbox.at[d], ss.at[d], rs.at[d], x_peer(d)).start()

    def z_start(inbox, outbox, total, xs, xr, ss, rs):
        for d in range(1, nx):
            remote(inbox.at[d], inbox.at[d], xs.at[d], xr.at[d], x_peer(d)).wait_recv()
        src = lax.div(lax.rem(row_id, nx * piece), piece) * (nz * piece)
        src = src + lax.div(row_id, nx * piece) * piece + lax.rem(row_id, piece)
        turn = jnp.where(src == col_id, 1.0, 0.0).astype(BF)
        stacked = inbox[...].reshape(length, inbox.shape[-1])
        moved = mm(turn, stacked).astype(BF)
        outbox[...] = moved.reshape(outbox.shape)
        total[0] = outbox[zz]
        for d in range(1, nz):
            remote(outbox.at[wrap(zz + d, nz)], total.at[d], ss.at[d], rs.at[d], z_peer(d)).start()

    def core_start(mine, zs, zr, ss, rs):
        for d in range(1, nz):
            remote(mine.at[d], mine.at[d], zs.at[d], zr.at[d], z_peer(d)).wait_recv()
        remote(mine, mine, ss, rs, other).start()

    def prepare():
        remote(hx_s, hx_o, hx_ss.at[0], hx_rs.at[0], other).start()
        ids = jnp.concatenate([pack_plan(m) for m in range(micro)], -1)
        idp_s[...] = ids.reshape(idp_s.shape)
        x_start(idp_s, idx_r, ix_ss.at[0], ix_rs.at[0])
        for kind in range(2):
            lt_s[kind, 0] = hx_s[kind].reshape(micro * length, width).T
        z_start(idx_r, idz_s, idt_s.at[core], ix_ss.at[0], ix_rs.at[0], iz_ss.at[0], iz_rs.at[0])
        remote(hx_s, hx_o, hx_ss.at[0], hx_rs.at[0], other).wait_recv()
        for kind in range(2):
            lt_s[kind, 1] = hx_o[kind].reshape(micro * length, width).T
        core_start(idt_s.at[core], iz_ss.at[0], iz_rs.at[0], ic_ss.at[0], ic_rs.at[0])
        remote(idt_s.at[1 - core], idt_s.at[1 - core], ic_ss.at[0], ic_rs.at[0], other).wait_recv()
        hits = jnp.zeros((own_rows, 1), F32)
        own_id = lax.broadcasted_iota(jnp.int32, (own_rows, length), 0).astype(F32)
        for c in range(2):
            for m in range(micro):
                both = idt_s[c, :, :, m * LANES:(m + 1) * LANES].reshape(length, LANES).astype(F32).T
                name = both[:1] * 32.0 + both[LANES // 2:LANES // 2 + 1] - 1.0
                hot = jnp.where(own_id == name, 1.0, 0.0)
                hits = hits + jnp.sum(hot, -1, keepdims=True)
                oh_s[:, (c * micro + m) * length:(c * micro + m + 1) * length] = hot.astype(BF)
        hits_ref[...] = jnp.broadcast_to(hits, hits_ref.shape)

    @pl.when(sec < ns - 1)
    def _():
        @pl.loop(0, micro)
        def _(m):
            forward(m)

    @pl.when(sec == ns - 1)
    def _():
        forward(0)

    pl.semaphore_wait(barrier, len(peers))

    early = ns // 2

    @pl.when(sec < early)
    def _():
        prepare()

    def hop(m):
        return remote(
            below_s.at[m], g_s.at[m], hop_ss.at[m], hop_rs.at[m],
            (wrap(sec + ns - 1, ns), smp, core),
        )

    def token(m, place):
        return remote(
            below_s.at[m], tk_s.at[m], tk_ss.at[m, place], tk_rs.at[m, 0],
            (1 if place == 0 else ns - 1, smp, core),
        )

    def token_on(m, place):
        span = pl.ds(place * (length // 2), length // 2)
        return remote(
            tk_s.at[m, span], tk_s.at[m, span], tk_ss.at[m, 0], tk_rs.at[m, place], (2, smp, core)
        )

    @pl.loop(0, micro)
    def _(m):
        @pl.when(sec == ns - 1)
        def _():
            @pl.when(m > 0)
            def _():
                forward(m)
            g_s[m] = og_ref[m]

        @pl.when(sec < ns - 1)
        def _():
            hop(m).wait_recv()

        backward(m)

        @pl.when(sec > 0)
        def _():
            hop(m).start()

        @pl.when(sec == 0)
        def _():
            tk_s[m] = below_s[m]
            token(m, 0).start()
            if ns > 2:
                token(m, 1).start()

    @pl.when(sec >= early)
    def _():
        prepare()

    @pl.loop(0, PARTS)
    def _(k):
        for m in range(micro):
            remote(d_s.at[1 - core, k, m], d_r.at[k, m], d_ss.at[k, m], d_rs.at[k, m], other).wait_recv()
        kind = jnp.minimum(k, 1)
        part = mm(lt_s[kind, 0], d_s[core, k].reshape(micro * length, half))
        part = part + mm(lt_s[kind, 1], d_r[k].reshape(micro * length, half))
        part = part.astype(BF)
        for z in range(nz):
            for x in range(nx):
                at = (z * nx + x) * rows
                gw_s[k, x, z * rows:(z + 1) * rows, :] = part[at:at + rows]
        for d in range(1, nx):
            remote(
                gw_s.at[k, wrap(xx + d, nx)], gx_r.at[k, d], gx_ss.at[k, d], gx_rs.at[k, d], x_peer(d)
            ).start()

    def get_tokens(m):
        if ns > 2:
            @pl.when((sec == 1) | (sec == 3))
            def _():
                token(m, 0).wait_recv()

            @pl.when(sec == 1)
            def _():
                token_on(m, 0).start()

            @pl.when(sec == 3)
            def _():
                token_on(m, 1).start()

            @pl.when(sec == 2)
            def _():
                token_on(m, 0).wait_recv()
                token_on(m, 1).wait_recv()
        else:
            @pl.when(sec == 1)
            def _():
                token(m, 0).wait_recv()
        packed = mm(p_s[m], tk_s[m]).astype(BF)
        tp_s[m] = packed.reshape(tp_s.shape[1:])
        x_start(tp_s.at[m], tx_r.at[m], ix_ss.at[1 + m], ix_rs.at[1 + m])

    get_tokens(0)

    @pl.when(sec == 0)
    def _():
        get_tokens(1)

    @pl.loop(0, PARTS)
    def _(k):
        total = gw_s[k, xx].astype(F32)
        for d in range(1, nx):
            remote(gx_r.at[k, d], gx_r.at[k, d], gx_ss.at[k, d], gx_rs.at[k, d], x_peer(d)).wait_recv()
            total = total + gx_r[k, d].astype(F32)
        total = total.astype(BF)
        for z in range(nz):
            gz_s[z, k] = total[z * rows:(z + 1) * rows]

    for d in range(1, nz):
        remote(gz_s.at[wrap(zz + d, nz)], gz_r.at[d], gz_ss.at[d], gz_rs.at[d], z_peer(d)).start()

    @pl.when(sec > 0)
    def _():
        get_tokens(1)

    for m in range(micro):
        z_start(
            tx_r.at[m], tz_s.at[m], tt_s.at[core, m],
            ix_ss.at[1 + m], ix_rs.at[1 + m], iz_ss.at[1 + m], iz_rs.at[1 + m],
        )

    total = gz_s[zz].astype(F32)
    for d in range(1, nz):
        remote(gz_r.at[d], gz_r.at[d], gz_ss.at[d], gz_rs.at[d], z_peer(d)).wait_recv()
        total = total + gz_r[d].astype(F32)
    f_s[core] = total.astype(BF)
    remote(f_s.at[core], f_s.at[core], f_ss.at[0], f_rs.at[0], other).start()

    for m in range(micro):
        core_start(tt_s.at[core, m], iz_ss.at[1 + m], iz_rs.at[1 + m], ic_ss.at[1 + m], ic_rs.at[1 + m])

    remote(f_s.at[1 - core], f_s.at[1 - core], f_ss.at[0], f_rs.at[0], other).wait_recv()
    tokens_all = micro * length * nz * nx * 2
    factor = float(tokens_all) ** (-0.5)
    for c in range(2):
        go_ref[:, c * half:(c + 1) * half] = f_s[c, 0].astype(F32) * factor
        for k in range(4):
            at = k * width + c * half
            gi_ref[:, at:at + half] = f_s[c, k + 1].astype(F32) * factor

    for m in range(micro):
        remote(
            tt_s.at[1 - core, m], tt_s.at[1 - core, m], ic_ss.at[1 + m], ic_rs.at[1 + m], other
        ).wait_recv()
    rg_ref[...] = mm(oh_s[...], tt_s[...].reshape(2 * micro * length, width))

    remote(hx_s, hx_o, hx_ss.at[0], hx_rs.at[0], other).wait_send()
    remote(f_s.at[core], f_s.at[core], f_ss.at[0], f_rs.at[0], other).wait_send()

    @pl.loop(0, PARTS)
    def _(k):
        for m in range(micro):
            remote(d_s.at[1 - core, k, m], d_r.at[k, m], d_ss.at[k, m], d_rs.at[k, m], other).wait_send()
        for d in range(1, nx):
            remote(
                gw_s.at[k, wrap(xx + d, nx)], gx_r.at[k, d], gx_ss.at[k, d], gx_rs.at[k, d], x_peer(d)
            ).wait_send()

    for d in range(1, nz):
        remote(gz_s.at[wrap(zz + d, nz)], gz_r.at[d], gz_ss.at[d], gz_rs.at[d], z_peer(d)).wait_send()
    for i in range(1 + micro):
        pack = idp_s if i == 0 else tp_s.at[i - 1]
        inbox = idx_r if i == 0 else tx_r.at[i - 1]
        outbox = idz_s if i == 0 else tz_s.at[i - 1]
        full = idt_s.at[core] if i == 0 else tt_s.at[core, i - 1]
        for d in range(1, nx):
            remote(
                pack.at[wrap(xx + d, nx)], inbox.at[d], ix_ss.at[i, d], ix_rs.at[i, d], x_peer(d)
            ).wait_send()
        for d in range(1, nz):
            remote(
                outbox.at[wrap(zz + d, nz)], full.at[d], iz_ss.at[i, d], iz_rs.at[i, d], z_peer(d)
            ).wait_send()
        remote(full, full, ic_ss.at[i], ic_rs.at[i], other).wait_send()
    for m in range(micro):
        @pl.when(sec > 0)
        def _():
            hop(m).wait_send()

        @pl.when(sec == 0)
        def _():
            token(m, 0).wait_send()
            if ns > 2:
                token(m, 1).wait_send()

        if ns > 2:
            @pl.when(sec == 1)
            def _():
                token_on(m, 0).wait_send()

            @pl.when(sec == 3)
            def _():
                token_on(m, 1).wait_send()


def exchange(dims, x, og, w_in, w_out, owner, slot, own_rows):
    ns, nz, nx, cap = dims
    micro, length, width = x.shape
    half = width // 2
    rows = width // (nz * nx)
    dma = pltpu.SemaphoreType.DMA
    vm = pltpu.VMEM
    lx, lz = length // nx, length // nz
    streams = 1 + micro
    wide = LANES * micro
    scratch = [
        vm((micro, length, width), F32),
        vm((micro, length, 1), F32),
        vm((micro, 4, length, width), BF),
        vm((micro, 4, length, width), F32),
        vm((micro, HEADS, length, length), BF),
        vm((micro, HEADS, length, length), F32),
        vm((micro, length, width), F32),
        vm((micro, length, 1), F32),
        vm((2, micro, length, width), BF),
        vm((2, micro, length, width), BF),
        vm((2, 2, width, micro * length), BF),
        vm((micro, length, width), BF),
        vm((micro, length, width), BF),
        vm((2, PARTS, micro, length, half), BF),
        vm((PARTS, micro, length, half), BF),
        vm((PARTS, nx, nz * rows, half), BF),
        vm((PARTS, nx, nz * rows, half), BF),
        vm((nz, PARTS, rows, half), BF),
        vm((nz, PARTS, rows, half), BF),
        vm((2, PARTS, rows, half), BF),
        vm((micro, length, length), BF),
        vm((micro, length, width), BF),
        vm((nx, lx, wide), BF),
        vm((nx, lx, wide), BF),
        vm((nz, lz, wide), BF),
        vm((2, nz, lz, wide), BF),
        vm((micro, nx, lx, width), BF),
        vm((micro, nx, lx, width), BF),
        vm((micro, nz, lz, width), BF),
        vm((2, micro, nz, lz, width), BF),
        vm((own_rows, 2 * micro * length), BF),
        dma((micro,)), dma((micro,)), dma((1,)), dma((1,)),
        dma((PARTS, micro)), dma((PARTS, micro)),
        dma((PARTS, nx)), dma((PARTS, nx)),
        dma((nz,)), dma((nz,)), dma((1,)), dma((1,)),
        dma((micro, 2)), dma((micro, 2)),
        dma((streams, nx)), dma((streams, nx)),
        dma((streams, nz)), dma((streams, nz)),
        dma((streams,)), dma((streams,)),
    ]
    return pl.pallas_call(
        functools.partial(kernel, dims),
        out_shape=(
            jax.ShapeDtypeStruct((own_rows, width), F32),
            jax.ShapeDtypeStruct((own_rows, LANES), F32),
            jax.ShapeDtypeStruct((rows, 4 * width), F32),
            jax.ShapeDtypeStruct((rows, width), F32),
        ),
        in_specs=[pl.BlockSpec(memory_space=pltpu.VMEM)] * 6,
        out_specs=[pl.BlockSpec(memory_space=pltpu.VMEM)] * 4,
        scratch_shapes=scratch,
        compiler_params=pltpu.CompilerParams(
            collective_id=0, has_side_effects=True, vmem_limit_bytes=48 << 20
        ),
    )(x, og, w_in, w_out, owner, slot)


def local(nz, nx, saved_input, out_grad, w_in, w_out, item_owner, item_slot, table, moment, second):
    ns = lax.axis_size("section")
    micro, length, width = out_grad.shape[0], out_grad.shape[2], out_grad.shape[3]
    owners = ns * nz * nx
    cap = max(2, 2 * BLOCK // owners)
    row_grad, hits, grad_in, grad_out = exchange(
        (ns, nz, nx, cap),
        saved_input[0, :, 0],
        out_grad[:, 0],
        w_in[0],
        w_out[0],
        item_owner.reshape(micro, length),
        item_slot.reshape(micro, length),
        table.shape[0],
    )
    hits = hits[:, 0]
    touched = hits > 0.5
    moment_new = jnp.where(
        touched[:, None], BETA_ONE * moment + (1.0 - BETA_ONE) * row_grad, moment
    )
    second_new = jnp.where(
        touched, BETA_TWO * second + (1.0 - BETA_TWO) * jnp.mean(row_grad * row_grad, -1), second
    )
    table_new = jnp.where(
        touched[:, None],
        table - STEP_SIZE * moment_new / (jnp.sqrt(second_new)[:, None] + ADAM_EPS),
        table,
    )
    return (grad_in[None], grad_out[None], table_new, moment_new, second_new)


def solution(mesh):
    samples = mesh.shape["sample"]
    nx = 4 if samples >= 16 else 2
    nz = samples // nx
    placed = (
        P("section", None, ("sample", "replica"), None, None),
        P(None, ("sample", "replica"), None, None),
        P("section", None, None),
        P("section", None, None),
        P(("sample", "replica"), None, None, None),
        P(("sample", "replica"), None, None),
        P(("section", "sample"), None),
        P(("section", "sample"), None),
        P(("section", "sample")),
    )
    return jax.shard_map(
        functools.partial(local, nz, nx),
        mesh=mesh,
        in_specs=placed,
        out_specs=(
            P("section", "sample", None),
            P("section", "sample", None),
            P(("section", "sample"), None),
            P(("section", "sample"), None),
            P(("section", "sample")),
        ),
        check_vma=False,
    )
```

time: 708 us -> 79 us (0.11)
  waiting for transfers between devices: 418 us -> 0 us
  local copies, waits for them, and re-layouts: 110 us -> 7.16 us
  Pallas kernels: 0 us -> 68.3 us
  matrix products: 67.1 us -> 0 us
  other arithmetic: 43.7 us -> 2.56 us
  starting transfers between devices: 35.9 us -> 0 us
  between operations: 16.4 us -> 0.67 us
  blocking collectives: 9.92 us -> 0 us
    reduce_scatter x2 -> x0, waiting for transfers between devices: 366 us -> none  [the longest x1 216 us: local(): lax.psum_scatter(acc_out.astype(jnp.bfloat16), 'sample', scatter_dimensio...]
    pallas_call x0 -> x1, Pallas kernels: none -> 68.3 us  [exchange(): pl.pallas_call(functools.partial(kernel, dims), out_shape=(jax.ShapeDtype...]
    dot_general x58 -> x0, matrix products: 67.1 us -> none  [the longest x5 20.6 us: layer_back(): grad_in = jnp.dot(flat_in.T, grad_pre, preferred_element_type=jnp.float32)]
    reshape x34 -> x0, local copies, waits for them, and re-layouts: 49.1 us -> none  [the longest x4 11.7 us: layer_back(): slopes = silu_slope(pre_act, pre_sig).reshape(batch, length, 4, width)]
    slice x14 -> x0, local copies, waits for them, and re-layouts: 35 us -> none  [the longest x5 21.8 us: layer_back(): slopes[:, :, k]]
    all_to_all x2 -> x0, starting transfers between devices: 29.8 us -> none  [the longest x1 16.6 us: local(): lax.all_to_all(sent_slots, ('section', 'sample'), split_axis=0, concat_ax...]
    psum x1 -> x0, waiting for transfers between devices: 26.9 us -> none  [local(): lax.psum(share_in.astype(jnp.bfloat16), 'replica').astype(jnp.float32)]
    convert_element_type x26 -> x0, other arithmetic: 23 us -> none  [the longest x20 21.7 us: layer_back(): (pieces[k] * slopes[:, :, k]).astype(jnp.bfloat16)]
  transfers between devices with their start and end apart: 9 -> 0, of which waited for: 8 -> 0; matrix products, arithmetic and copies ran while one was open for 15% -> 0% of each run, Pallas kernels for 0% -> 0%
where the time goes in v1:
time: 79 us; the launch traced here: 78.7 us
  Pallas kernels  68.3 us (86%)
  local copies, waits for them, and re-layouts  7.16 us (9%)
  other arithmetic  2.56 us (3%)
    pallas_call x1, Pallas kernels, exchange(): pl.pallas_call(functools.partial(kernel, dims), out_shape=(jax.ShapeDtype...  68.3 us
    unnamed x20, local copies, waits for them, and re-layouts  7.16 us
    select_n x1, other arithmetic, local(): jnp.where(touched[:, None], table - STEP_SIZE * moment_new / (jnp.sqrt(se...  1.68 us

profile of v1, /device:TPU:1, one launch (start us, length us, event | category | flops | bytes accessed | tf_op | source)
XLA Modules:
  0.0 78.7 jit_solution(7979906886590798565)
XLA Ops:
  0.6 0.0 copy-start
  0.6 1.6 %copy-done = bf16[1,512,2048]{2,1,0:T(8,128)(2,1)S(1)} copy-done((bf16[1,512,2048]{2,1,0:T(8,128)(2,1)S(1)}, bf16[1,512,2048]{2,1,0:T(8,128)(2,1)}, u32[]{:S(2)}) %copy-start) | copy-done | bytes 2097176
  2.2 0.0 copy-start.1
  2.2 1.0 %copy-done.1 = bf16[1,512,512]{2,1,0:T(8,128)(2,1)S(1)} copy-done((bf16[1,512,512]{2,1,0:T(8,128)(2,1)S(1)}, bf16[1,512,512]{2,1,0:T(8,128)(2,1)}, u32[]{:S(2)}) %copy-start.1) | copy-done | bytes 524312
  3.3 0.0 copy-start.2
  3.3 0.9 %copy-done.2 = bf16[1,2,1,128,512]{4,3,2,1,0:T(8,128)(2,1)S(1)} copy-done((bf16[1,2,1,128,512]{4,3,2,1,0:T(8,128)(2,1)S(1)}, bf16[1,2,1,128,512]{4,3,2,1,0:T(8,128)(2,1)}, u32[]{:S(2)}) %copy-start.2) | copy-done | bytes 262168
  4.2 0.0 copy-start.3
  4.2 0.9 %copy-done.3 = bf16[2,1,128,512]{3,2,1,0:T(8,128)(2,1)S(1)} copy-done((bf16[2,1,128,512]{3,2,1,0:T(8,128)(2,1)S(1)}, bf16[2,1,128,512]{3,2,1,0:T(8,128)(2,1)}, u32[]{:S(2)}) %copy-start.3) | copy-done | bytes 262168
  5.2 0.0 copy-start.4
  5.2 0.7 copy-done.4
  5.8 0.0 copy-start.5
  5.9 0.7 copy-done.5
  6.5 0.0 copy-start.8
  6.5 0.0 copy-start.6
  6.5 0.0 copy-start.7
  6.5 68.3 %shard_map.128 = (f32[512,512]{1,0:T(8,128)S(1)}, f32[512,128]{1,0:T(8,128)S(1)}, f32[16,2048]{1,0:T(8,128)S(1)}, f32[16,512]{1,0:T(8,128)S(1)}) custom-call(bf16[2,128,512]{2,1,0:T(8,128)(2,1)S(1)} %bitcast.10, bf16[2,128,512]{2,1,0:T(8,128)(2,1)S(1)} %bitcast.11, bf16[512,2048]{1,0:T(8,128)(2,1)S(1)} %bitcast.8, bf16[512,512]{1,0:T(8,128)(2,1)S(1)} %bitcast.9, ...), custom_call_target="tpu_custom_call" | custom-call | tf_op jit(solution)/shard_map/pallas_call | solution.py:491
  74.9 0.1 fusion
  75.0 0.2 multiply_reduce_fusion
  75.2 0.0 copy-done.8
  75.2 0.6 sqrt_add_fusion
  75.8 0.0 copy-done.6
  75.8 0.0 copy-done.7
  75.8 1.7 %subtract_select_fusion = (f32[512,512]{1,0:T(8,128)}, f32[512,512]{1,0:T(8,128)}) fusion(f32[512,512]{1,0:T(8,128)S(1)} %copy-done.6, f32[512]{0:T(512)S(1)} %get-tuple-element.15, pred[512]{0:T(512)(128)(4,1)S(1)} %fusion, f32[512,512]{1,0:T(8,128)S(1)} %copy-done.7, f32[512,512]{1,0:T(8,128)S(1)} %get-tuple-element.12), kind=kLoop, calls=%fused_computation | loop fusion | flops 2097152 | bytes 5245440 | tf_op jit(solution)/shard_map/jit(_where)/select_n | solution.py:531
  77.4 0.7 copy.16
  78.1 0.6 copy.17
Async XLA Ops:
  0.6 1.6 %copy-start = (bf16[1,512,2048]{2,1,0:T(8,128)(2,1)S(1)}, bf16[1,512,2048]{2,1,0:T(8,128)(2,1)}, u32[]{:S(2)}) copy-start(bf16[1,512,2048]{2,1,0:T(8,128)(2,1)} %param.11) | copy-start | bytes 6291460
  2.2 1.0 %copy-start.1 = (bf16[1,512,512]{2,1,0:T(8,128)(2,1)S(1)}, bf16[1,512,512]{2,1,0:T(8,128)(2,1)}, u32[]{:S(2)}) copy-start(bf16[1,512,512]{2,1,0:T(8,128)(2,1)} %param.12) | copy-start | bytes 1572868
  3.3 0.9 %copy-start.2 = (bf16[1,2,1,128,512]{4,3,2,1,0:T(8,128)(2,1)S(1)}, bf16[1,2,1,128,512]{4,3,2,1,0:T(8,128)(2,1)}, u32[]{:S(2)}) copy-start(bf16[1,2,1,128,512]{4,3,2,1,0:T(8,128)(2,1)} %param.9) | copy-start | bytes 786436
  4.2 0.9 %copy-start.3 = (bf16[2,1,128,512]{3,2,1,0:T(8,128)(2,1)S(1)}, bf16[2,1,128,512]{3,2,1,0:T(8,128)(2,1)}, u32[]{:S(2)}) copy-start(bf16[2,1,128,512]{3,2,1,0:T(8,128)(2,1)} %param.10) | copy-start | bytes 786436
  5.2 0.7 copy-start.4
  5.8 0.7 copy-start.5
  6.5 68.6 %copy-start.8 = (f32[512]{0:T(512)S(1)}, f32[512]{0:T(512)}, u32[]{:S(2)}) copy-start(f32[512]{0:T(512)} %param.17) | copy-start | bytes 6148
  6.5 69.2 %copy-start.6 = (f32[512,512]{1,0:T(8,128)S(1)}, f32[512,512]{1,0:T(8,128)}, u32[]{:S(2)}) copy-start(f32[512,512]{1,0:T(8,128)} %param.15) | copy-start | bytes 3145732
  6.5 69.2 %copy-start.7 = (f32[512,512]{1,0:T(8,128)S(1)}, f32[512,512]{1,0:T(8,128)}, u32[]{:S(2)}) copy-start(f32[512,512]{1,0:T(8,128)} %param.16) | copy-start | bytes 3145732

commit v2 on v1

--- a/solution.py
+++ b/solution.py
@@ -54,13 +54,15 @@
 
 def kernel(
     dims,
-    x_ref, og_ref, win_ref, wout_ref, owner_ref, slot_ref,
-    rg_ref, hits_ref, gi_ref, go_ref,
+    x_hbm, og_hbm, win_hbm, wout_hbm, owner_hbm, slot_hbm,
+    rg_hbm, hits_hbm, f_hbm,
+    rg_ref, hits_ref, x_ref, win_ref, wout_ref, owner_ref, slot_ref,
     xn_s, rx_s, act_s, slope_s, w_s, zs_s, mn_s, rm_s,
     hx_s, hx_o, lt_s, g_s, below_s, d_s, d_r,
-    gw_s, gx_r, gz_s, gz_r, f_s,
+    gw_s, g1_r, g2_s, g2_r, gz_s, gz_r, f_s,
     p_s, tk_s, idp_s, idx_r, idz_s, idt_s, tp_s, tx_r, tz_s, tt_s, oh_s,
-    hop_ss, hop_rs, hx_ss, hx_rs, d_ss, d_rs, gx_ss, gx_rs, gz_ss, gz_rs, f_ss, f_rs,
+    in_ss, out_ss, hop_ss, hop_rs, hx_ss, hx_rs, d_ss, d_rs,
+    g1_ss, g1_rs, g2_ss, g2_rs, gz_ss, gz_rs, f_ss, f_rs,
     tk_ss, tk_rs, ix_ss, ix_rs, iz_ss, iz_rs, ic_ss, ic_rs,
 ):
     ns, nz, nx, cap = dims
@@ -69,7 +71,7 @@
     hs = width // HEADS
     scale = hs ** (-0.5)
     rows = width // (nz * nx)
-    own_rows = rg_ref.shape[0]
+    own_rows = rg_hbm.shape[0]
     piece = length // (nz * nx)
     sec = lax.axis_index("section")
     smp = lax.axis_index("sample")
@@ -91,6 +93,30 @@
         return pltpu.make_async_remote_copy(
             src_ref=src, dst_ref=dst, send_sem=ss, recv_sem=rs, device_id=dev, device_id_type=MESH
         )
+
+    def load(i, src, dst):
+        return pltpu.make_async_copy(src, dst, in_ss.at[i])
+
+    def save(i, src, dst):
+        return pltpu.make_async_copy(src, dst, out_ss.at[i])
+
+    def save_rows(b):
+        at = pl.ds(b * LANES, LANES)
+        return save(2 + b, rg_ref.at[at], rg_hbm.at[at])
+
+    loads = [
+        load(i, src, dst)
+        for i, (src, dst) in enumerate((
+            (x_hbm, x_ref), (win_hbm, win_ref), (wout_hbm, wout_ref),
+            (owner_hbm, owner_ref), (slot_hbm, slot_ref),
+        ))
+    ]
+    for one in loads:
+        one.start()
+
+    @pl.when(sec == ns - 1)
+    def _():
+        load(5, og_hbm, g_s).start()
 
     barrier = pltpu.get_barrier_semaphore()
     peers = [other]
@@ -129,10 +155,51 @@
         rm_s[m] = rm
         hx_s[0, m] = (mn * act_s[m, 0].astype(F32)).astype(BF)
 
+    first = jnp.where(core == 0, 1, nx - 1)
+    second = nx - first
+
+    def flip(v, mask):
+        pair = v + 1 - 2 * lax.rem(v, 2)
+        return jnp.where(mask == 1, pair, nx - 1 - v)
+
+    def x_at(x):
+        return (sec, zz * nx + x, core)
+
+    def g1_copy(k):
+        return remote(
+            gw_s.at[k, pl.ds(2, 2)], g1_r.at[k], g1_ss.at[k], g1_rs.at[k], x_at(flip(xx, first))
+        )
+
+    def g2_copy(k):
+        return remote(g2_s.at[k], g2_r.at[k], g2_ss.at[k], g2_rs.at[k], x_at(flip(xx, second)))
+
+    def gz_copy(k, d):
+        return remote(
+            gz_s.at[wrap(zz + d, nz), k], gz_r.at[d, k], gz_ss.at[d, k], gz_rs.at[d, k], z_peer(d)
+        )
+
+    def d_copy(k, m):
+        return remote(d_s.at[1 - core, k, m], d_r.at[k, m], d_ss.at[k, m], d_rs.at[k, m], other)
+
+    def gradient(k, kind):
+        for m in range(micro):
+            d_copy(k, m).wait_recv()
+        part = mm(lt_s[kind, 0], d_s[core, k].reshape(micro * length, half))
+        part = part + mm(lt_s[kind, 1], d_r[k].reshape(micro * length, half))
+        part = part.astype(BF)
+        for x in range(nx):
+            slot = jnp.where(
+                xx == x, 0, jnp.where(flip(xx, second) == x, 1, jnp.where(flip(xx, first) == x, 2, 3))
+            )
+            for z in range(nz):
+                at = (z * nx + x) * rows
+                gw_s[k, slot, z * rows:(z + 1) * rows, :] = part[at:at + rows]
+        g1_copy(k).start()
+
     def keep(m, k, value):
         d_s[0, k, m] = value[:, :half]
         d_s[1, k, m] = value[:, half:]
-        remote(d_s.at[1 - core, k, m], d_r.at[k, m], d_ss.at[k, m], d_rs.at[k, m], other).start()
+        d_copy(k, m).start()
 
     def backward(m):
         g = g_s[m]
@@ -154,6 +221,12 @@
         for k, part in enumerate((dv, dq, dk)):
             dpre.append((jnp.concatenate(part, -1) * slope_s[m, k + 1]).astype(BF))
             keep(m, k + 2, dpre[-1])
+
+        @pl.when((sec == 0) & (m == micro - 1))
+        def _():
+            gradient(0, 0)
+            gradient(1, 1)
+
         dxn = mm_nt(dpre[0], win_ref[:, :width])
         for k in range(1, 4):
             dxn = dxn + mm_nt(dpre[k], win_ref[:, k * width:(k + 1) * width])
@@ -223,7 +296,13 @@
                 hot = jnp.where(own_id == name, 1.0, 0.0)
                 hits = hits + jnp.sum(hot, -1, keepdims=True)
                 oh_s[:, (c * micro + m) * length:(c * micro + m + 1) * length] = hot.astype(BF)
-        hits_ref[...] = jnp.broadcast_to(hits, hits_ref.shape)
+        for b in range(own_rows // LANES):
+            column = hits[b * LANES:(b + 1) * LANES]
+            hits_ref[b:b + 1, :] = jnp.broadcast_to(column, (LANES, LANES)).T[:1]
+        save(0, hits_ref, hits_hbm).start()
+
+    loads[0].wait()
+    loads[1].wait()
 
     @pl.when(sec < ns - 1)
     def _():
@@ -235,6 +314,13 @@
     def _():
         forward(0)
 
+    for one in loads[2:]:
+        one.wait()
+
+    @pl.when(sec == ns - 1)
+    def _():
+        load(5, og_hbm, g_s).wait()
+
     pl.semaphore_wait(barrier, len(peers))
 
     early = ns // 2
@@ -261,14 +347,16 @@
             tk_s.at[m, span], tk_s.at[m, span], tk_ss.at[m, 0], tk_rs.at[m, place], (2, smp, core)
         )
 
+    def pack(m):
+        packed = mm(p_s[m], tk_s[m]).astype(BF)
+        tp_s[m] = packed.reshape(tp_s.shape[1:])
+        x_start(tp_s.at[m], tx_r.at[m], ix_ss.at[1 + m], ix_rs.at[1 + m])
+
     @pl.loop(0, micro)
     def _(m):
-        @pl.when(sec == ns - 1)
-        def _():
-            @pl.when(m > 0)
-            def _():
-                forward(m)
-            g_s[m] = og_ref[m]
+        @pl.when((sec == ns - 1) & (m > 0))
+        def _():
+            forward(m)
 
         @pl.when(sec < ns - 1)
         def _():
@@ -286,27 +374,15 @@
             token(m, 0).start()
             if ns > 2:
                 token(m, 1).start()
+            pack(m)
 
     @pl.when(sec >= early)
     def _():
         prepare()
 
-    @pl.loop(0, PARTS)
+    @pl.loop(jnp.where(sec == 0, 2, 0), PARTS)
     def _(k):
-        for m in range(micro):
-            remote(d_s.at[1 - core, k, m], d_r.at[k, m], d_ss.at[k, m], d_rs.at[k, m], other).wait_recv()
-        kind = jnp.minimum(k, 1)
-        part = mm(lt_s[kind, 0], d_s[core, k].reshape(micro * length, half))
-        part = part + mm(lt_s[kind, 1], d_r[k].reshape(micro * length, half))
-        part = part.astype(BF)
-        for z in range(nz):
-            for x in range(nx):
-                at = (z * nx + x) * rows
-                gw_s[k, x, z * rows:(z + 1) * rows, :] = part[at:at + rows]
-        for d in range(1, nx):
-            remote(
-                gw_s.at[k, wrap(xx + d, nx)], gx_r.at[k, d], gx_ss.at[k, d], gx_rs.at[k, d], x_peer(d)
-            ).start()
+        gradient(k, jnp.minimum(k, 1))
 
     def get_tokens(m):
         if ns > 2:
@@ -327,66 +403,73 @@
                 token_on(m, 0).wait_recv()
                 token_on(m, 1).wait_recv()
         else:
-            @pl.when(sec == 1)
-            def _():
-                token(m, 0).wait_recv()
-        packed = mm(p_s[m], tk_s[m]).astype(BF)
-        tp_s[m] = packed.reshape(tp_s.shape[1:])
-        x_start(tp_s.at[m], tx_r.at[m], ix_ss.at[1 + m], ix_rs.at[1 + m])
-
-    get_tokens(0)
-
-    @pl.when(sec == 0)
-    def _():
-        get_tokens(1)
-
-    @pl.loop(0, PARTS)
-    def _(k):
-        total = gw_s[k, xx].astype(F32)
-        for d in range(1, nx):
-            remote(gx_r.at[k, d], gx_r.at[k, d], gx_ss.at[k, d], gx_rs.at[k, d], x_peer(d)).wait_recv()
-            total = total + gx_r[k, d].astype(F32)
-        total = total.astype(BF)
-        for z in range(nz):
-            gz_s[z, k] = total[z * rows:(z + 1) * rows]
-
-    for d in range(1, nz):
-        remote(gz_s.at[wrap(zz + d, nz)], gz_r.at[d], gz_ss.at[d], gz_rs.at[d], z_peer(d)).start()
-
-    @pl.when(sec > 0)
-    def _():
-        get_tokens(1)
-
-    for m in range(micro):
-        z_start(
-            tx_r.at[m], tz_s.at[m], tt_s.at[core, m],
-            ix_ss.at[1 + m], ix_rs.at[1 + m], iz_ss.at[1 + m], iz_rs.at[1 + m],
+            token(m, 0).wait_recv()
+        pack(m)
+
+    def by_section(at_zero, at_one, at_rest):
+        return jnp.where(sec == 0, at_zero, jnp.where(sec == 1, at_one, at_rest))
+
+    def on_step(step, places, action):
+        start = [by_section(*place) for place in places]
+
+        @pl.when((step == start[0]) | (step == start[1]))
+        def _():
+            action(jnp.where(step == start[1], 1, 0))
+
+    @pl.loop(0, 11)
+    def _(step):
+        @pl.when(step < PARTS)
+        def _():
+            g1_copy(step).wait_recv()
+            total = gw_s[step, 1].astype(F32) + g1_r[step, 1].astype(F32)
+            g2_s[step] = total.astype(BF)
+            g2_copy(step).start()
+
+        @pl.when((step > 0) & (step <= PARTS))
+        def _():
+            k = step - 1
+            g2_copy(k).wait_recv()
+            total = gw_s[k, 0].astype(F32) + g1_r[k, 0].astype(F32) + g2_r[k].astype(F32)
+            total = total.astype(BF)
+            for z in range(nz):
+                gz_s[z, k] = total[z * rows:(z + 1) * rows]
+            for d in range(1, nz):
+                gz_copy(k, d).start()
+
+        on_step(step, ((-1, 2, 5), (-1, 5, 7)), get_tokens)
+        on_step(
+            step, ((1, 3, 6), (2, 6, 8)),
+            lambda m: z_start(
+                tx_r.at[m], tz_s.at[m], tt_s.at[core, m],
+                ix_ss.at[1 + m], ix_rs.at[1 + m], iz_ss.at[1 + m], iz_rs.at[1 + m],
+            ),
+        )
+        on_step(
+            step, ((4, 7, 9), (5, 8, 10)),
+            lambda m: core_start(
+                tt_s.at[core, m], iz_ss.at[1 + m], iz_rs.at[1 + m], ic_ss.at[1 + m], ic_rs.at[1 + m]
+            ),
         )
 
     total = gz_s[zz].astype(F32)
     for d in range(1, nz):
-        remote(gz_r.at[d], gz_r.at[d], gz_ss.at[d], gz_rs.at[d], z_peer(d)).wait_recv()
+        for k in range(PARTS):
+            gz_copy(k, d).wait_recv()
         total = total + gz_r[d].astype(F32)
     f_s[core] = total.astype(BF)
     remote(f_s.at[core], f_s.at[core], f_ss.at[0], f_rs.at[0], other).start()
-
-    for m in range(micro):
-        core_start(tt_s.at[core, m], iz_ss.at[1 + m], iz_rs.at[1 + m], ic_ss.at[1 + m], ic_rs.at[1 + m])
-
-    remote(f_s.at[1 - core], f_s.at[1 - core], f_ss.at[0], f_rs.at[0], other).wait_recv()
-    tokens_all = micro * length * nz * nx * 2
-    factor = float(tokens_all) ** (-0.5)
-    for c in range(2):
-        go_ref[:, c * half:(c + 1) * half] = f_s[c, 0].astype(F32) * factor
-        for k in range(4):
-            at = k * width + c * half
-            gi_ref[:, at:at + half] = f_s[c, k + 1].astype(F32) * factor
 
     for m in range(micro):
         remote(
             tt_s.at[1 - core, m], tt_s.at[1 - core, m], ic_ss.at[1 + m], ic_rs.at[1 + m], other
         ).wait_recv()
-    rg_ref[...] = mm(oh_s[...], tt_s[...].reshape(2 * micro * length, width))
+    tokens = tt_s[...].reshape(2 * micro * length, width)
+    for b in range(own_rows // LANES):
+        at = slice(b * LANES, (b + 1) * LANES)
+        rg_ref[at, :] = mm(oh_s[at, :], tokens)
+        save_rows(b).start()
+    remote(f_s.at[1 - core], f_s.at[1 - core], f_ss.at[0], f_rs.at[0], other).wait_recv()
+    save(1, f_s, f_hbm).start()
 
     remote(hx_s, hx_o, hx_ss.at[0], hx_rs.at[0], other).wait_send()
     remote(f_s.at[core], f_s.at[core], f_ss.at[0], f_rs.at[0], other).wait_send()
@@ -394,22 +477,20 @@
     @pl.loop(0, PARTS)
     def _(k):
         for m in range(micro):
-            remote(d_s.at[1 - core, k, m], d_r.at[k, m], d_ss.at[k, m], d_rs.at[k, m], other).wait_send()
-        for d in range(1, nx):
-            remote(
-                gw_s.at[k, wrap(xx + d, nx)], gx_r.at[k, d], gx_ss.at[k, d], gx_rs.at[k, d], x_peer(d)
-            ).wait_send()
-
-    for d in range(1, nz):
-        remote(gz_s.at[wrap(zz + d, nz)], gz_r.at[d], gz_ss.at[d], gz_rs.at[d], z_peer(d)).wait_send()
+            d_copy(k, m).wait_send()
+        g1_copy(k).wait_send()
+        g2_copy(k).wait_send()
+        for d in range(1, nz):
+            gz_copy(k, d).wait_send()
+
     for i in range(1 + micro):
-        pack = idp_s if i == 0 else tp_s.at[i - 1]
+        pack_from = idp_s if i == 0 else tp_s.at[i - 1]
         inbox = idx_r if i == 0 else tx_r.at[i - 1]
         outbox = idz_s if i == 0 else tz_s.at[i - 1]
         full = idt_s.at[core] if i == 0 else tt_s.at[core, i - 1]
         for d in range(1, nx):
             remote(
-                pack.at[wrap(xx + d, nx)], inbox.at[d], ix_ss.at[i, d], ix_rs.at[i, d], x_peer(d)
+                pack_from.at[wrap(xx + d, nx)], inbox.at[d], ix_ss.at[i, d], ix_rs.at[i, d], x_peer(d)
             ).wait_send()
         for d in range(1, nz):
             remote(
@@ -435,6 +516,83 @@
             @pl.when(sec == 3)
             def _():
                 token_on(m, 1).wait_send()
+
+    save(0, hits_ref, hits_hbm).wait()
+    save(1, f_s, f_hbm).wait()
+    for b in range(own_rows // LANES):
+        save_rows(b).wait()
+
+
+def finish(
+    factor,
+    rg_hbm, hits_hbm, f_hbm, table_in, moment_in, second_in,
+    gi_hbm, go_hbm, table_hbm, moment_hbm, second_hbm,
+    rg_ref, hits_ref, f_ref, table_ref, moment_ref, second_ref, gi_s, go_s, table_s, moment_s, second_s, in_sems, sems,
+):
+    half = f_ref.shape[-1]
+    width = 2 * half
+    blocks = rg_ref.shape[0] // LANES
+
+    copies = []
+
+    loads = [
+        pltpu.make_async_copy(src, dst, in_sems.at[i])
+        for i, (src, dst) in enumerate(((hits_hbm, hits_ref), (second_in, second_ref), (f_hbm, f_ref)))
+    ]
+
+    def row_loads(b):
+        at = pl.ds(b * LANES, LANES)
+        pairs = ((rg_hbm, rg_ref), (moment_in, moment_ref), (table_in, table_ref))
+        return [
+            pltpu.make_async_copy(src.at[at], dst.at[at], in_sems.at[3 + 3 * b + i])
+            for i, (src, dst) in enumerate(pairs)
+        ]
+
+    loads[0].start()
+    loads[1].start()
+    for b in range(blocks):
+        for load in row_loads(b):
+            load.start()
+    loads[2].start()
+    loads[0].wait()
+    loads[1].wait()
+
+    def put(src, dst):
+        copy = pltpu.make_async_copy(src, dst, sems.at[len(copies)])
+        copy.start()
+        copies.append(copy)
+
+    for b in range(blocks):
+        at = pl.ds(b * LANES, LANES)
+        for load in row_loads(b):
+            load.wait()
+        grad = rg_ref[at, :]
+        hit = jnp.broadcast_to(hits_ref[b:b + 1, :], (LANES, LANES)).T > 0.5
+        wide = jnp.concatenate([hit] * (width // LANES), -1)
+        square = jnp.mean(grad * grad, -1, keepdims=True)
+        square = jnp.broadcast_to(square, (LANES, LANES))
+        old = jnp.broadcast_to(second_ref[b:b + 1, :], (LANES, LANES)).T
+        new = jnp.where(hit, BETA_TWO * old + (1.0 - BETA_TWO) * square, old)
+        second_s[b:b + 1, :] = new.T[:1]
+        old_moment = moment_ref[at, :]
+        moment = jnp.where(wide, BETA_ONE * old_moment + (1.0 - BETA_ONE) * grad, old_moment)
+        moment_s[at, :] = moment
+        put(moment_s.at[at], moment_hbm.at[at])
+        old_table = table_ref[at, :]
+        below = jnp.concatenate([jnp.sqrt(new) + ADAM_EPS] * (width // LANES), -1)
+        table_s[at, :] = jnp.where(wide, old_table - STEP_SIZE * moment / below, old_table)
+        put(table_s.at[at], table_hbm.at[at])
+    put(second_s, second_hbm)
+    loads[2].wait()
+    for c in range(2):
+        go_s[:, c * half:(c + 1) * half] = f_ref[c, 0].astype(F32) * factor
+        for k in range(4):
+            at = k * width + c * half
+            gi_s[:, at:at + half] = f_ref[c, k + 1].astype(F32) * factor
+    put(go_s, go_hbm)
+    put(gi_s, gi_hbm)
+    for copy in copies:
+        copy.wait()
 
 
 def exchange(dims, x, og, w_in, w_out, owner, slot, own_rows):
@@ -448,6 +606,13 @@
     streams = 1 + micro
     wide = LANES * micro
     scratch = [
+        vm((own_rows, width), F32),
+        vm((own_rows // LANES, LANES), F32),
+        vm((micro, length, width), BF),
+        vm((width, 4 * width), BF),
+        vm((width, width), BF),
+        vm((micro, length), jnp.int32),
+        vm((micro, length), jnp.int32),
         vm((micro, length, width), F32),
         vm((micro, length, 1), F32),
         vm((micro, 4, length, width), BF),
@@ -464,7 +629,9 @@
         vm((2, PARTS, micro, length, half), BF),
         vm((PARTS, micro, length, half), BF),
         vm((PARTS, nx, nz * rows, half), BF),
-        vm((PARTS, nx, nz * rows, half), BF),
+        vm((PARTS, 2, nz * rows, half), BF),
+        vm((PARTS, nz * rows, half), BF),
+        vm((PARTS, nz * rows, half), BF),
         vm((nz, PARTS, rows, half), BF),
         vm((nz, PARTS, rows, half), BF),
         vm((2, PARTS, rows, half), BF),
@@ -479,10 +646,10 @@
         vm((micro, nz, lz, width), BF),
         vm((2, micro, nz, lz, width), BF),
         vm((own_rows, 2 * micro * length), BF),
-        dma((micro,)), dma((micro,)), dma((1,)), dma((1,)),
+        dma((6,)), dma((2 + own_rows // LANES,)), dma((micro,)), dma((micro,)), dma((1,)), dma((1,)),
         dma((PARTS, micro)), dma((PARTS, micro)),
-        dma((PARTS, nx)), dma((PARTS, nx)),
-        dma((nz,)), dma((nz,)), dma((1,)), dma((1,)),
+        dma((PARTS,)), dma((PARTS,)), dma((PARTS,)), dma((PARTS,)),
+        dma((nz, PARTS)), dma((nz, PARTS)), dma((1,)), dma((1,)),
         dma((micro, 2)), dma((micro, 2)),
         dma((streams, nx)), dma((streams, nx)),
         dma((streams, nz)), dma((streams, nz)),
@@ -492,15 +659,14 @@
         functools.partial(kernel, dims),
         out_shape=(
             jax.ShapeDtypeStruct((own_rows, width), F32),
-            jax.ShapeDtypeStruct((own_rows, LANES), F32),
-            jax.ShapeDtypeStruct((rows, 4 * width), F32),
-            jax.ShapeDtypeStruct((rows, width), F32),
+            jax.ShapeDtypeStruct((own_rows // LANES, LANES), F32),
+            jax.ShapeDtypeStruct((2, PARTS, rows, half), BF),
         ),
-        in_specs=[pl.BlockSpec(memory_space=pltpu.VMEM)] * 6,
-        out_specs=[pl.BlockSpec(memory_space=pltpu.VMEM)] * 4,
+        in_specs=[pl.BlockSpec(memory_space=pltpu.HBM)] * 6,
+        out_specs=[pl.BlockSpec(memory_space=pltpu.HBM)] * 3,
         scratch_shapes=scratch,
         compiler_params=pltpu.CompilerParams(
-            collective_id=0, has_side_effects=True, vmem_limit_bytes=48 << 20
+            collective_id=0, has_side_effects=True, vmem_limit_bytes=56 << 20
         ),
     )(x, og, w_in, w_out, owner, slot)
 
@@ -510,7 +676,9 @@
     micro, length, width = out_grad.shape[0], out_grad.shape[2], out_grad.shape[3]
     owners = ns * nz * nx
     cap = max(2, 2 * BLOCK // owners)
-    row_grad, hits, grad_in, grad_out = exchange(
+    own_rows = table.shape[0]
+    rows = width // (nz * nx)
+    row_grad, hits, grads = exchange(
         (ns, nz, nx, cap),
         saved_input[0, :, 0],
         out_grad[:, 0],
@@ -518,28 +686,28 @@
         w_out[0],
         item_owner.reshape(micro, length),
         item_slot.reshape(micro, length),
-        table.shape[0],
+        own_rows,
     )
-    hits = hits[:, 0]
-    touched = hits > 0.5
-    moment_new = jnp.where(
-        touched[:, None], BETA_ONE * moment + (1.0 - BETA_ONE) * row_grad, moment
-    )
-    second_new = jnp.where(
-        touched, BETA_TWO * second + (1.0 - BETA_TWO) * jnp.mean(row_grad * row_grad, -1), second
-    )
-    table_new = jnp.where(
-        touched[:, None],
-        table - STEP_SIZE * moment_new / (jnp.sqrt(second_new)[:, None] + ADAM_EPS),
-        table,
-    )
-    return (grad_in[None], grad_out[None], table_new, moment_new, second_new)
+    tokens = micro * length * nz * nx * lax.axis_size("replica")
+    lines = (own_rows // LANES, LANES)
+    shapes = [(rows, 4 * width), (rows, width), (own_rows, width), (own_rows, width), lines]
+    grad_in, grad_out, table_new, moment_new, second_new = pl.pallas_call(
+        functools.partial(finish, float(tokens) ** (-0.5)),
+        out_shape=[jax.ShapeDtypeStruct(shape, F32) for shape in shapes],
+        in_specs=[pl.BlockSpec(memory_space=pltpu.HBM)] * 6,
+        out_specs=[pl.BlockSpec(memory_space=pltpu.HBM)] * 5,
+        scratch_shapes=[pltpu.VMEM(part.shape, part.dtype) for part in (row_grad, hits, grads)]
+        + [pltpu.VMEM(shape, F32) for shape in shapes[2:]]
+        + [pltpu.VMEM(shape, F32) for shape in shapes]
+        + [pltpu.SemaphoreType.DMA((3 + 3 * lines[0],)), pltpu.SemaphoreType.DMA((2 * lines[0] + 3,))],
+        compiler_params=pltpu.CompilerParams(vmem_limit_bytes=56 << 20),
+    )(row_grad, hits, grads, table, moment, second.reshape(lines))
+    return (grad_in[None], grad_out[None], table_new, moment_new, second_new.reshape(own_rows))
 
 
 def solution(mesh):
-    samples = mesh.shape["sample"]
-    nx = 4 if samples >= 16 else 2
-    nz = samples // nx
+    nx = 4
+    nz = mesh.shape["sample"] // nx
     placed = (
         P("section", None, ("sample", "replica"), None, None),
         P(None, ("sample", "replica"), None, None),

time: 79 us -> 70.5 us (0.89)
  the two profiles are of different devices: /device:TPU:1 before, /device:TPU:17 now
where the time goes in v2:
time: 70.5 us; the launch traced here: 70.4 us
  Pallas kernels  69.7 us (99%)
    pallas_call x1, Pallas kernels, exchange(): pl.pallas_call(functools.partial(kernel, dims), out_shape=(jax.ShapeDtype...  66.7 us
    pallas_call x1, Pallas kernels, local(): pl.pallas_call(functools.partial(finish, float(tokens) ** (-0.5)), out_sh...  3.02 us

profile of v2, /device:TPU:17, one launch (start us, length us, event | category | flops | bytes accessed | tf_op | source)
XLA Modules:
  0.0 70.4 jit_solution(1667393650402505746)
XLA Ops:
  0.6 66.7 %shard_map.128 = (f32[512,512]{1,0:T(8,128)}, f32[4,128]{1,0:T(4,128)}, bf16[2,5,16,256]{3,2,1,0:T(8,128)(2,1)}) custom-call(bf16[2,128,512]{2,1,0:T(8,128)(2,1)} %bitcast.12, bf16[2,128,512]{2,1,0:T(8,128)(2,1)} %bitcast.13, bf16[512,2048]{1,0:T(8,128)(2,1)} %bitcast.10, bf16[512,512]{1,0:T(8,128)(2,1)} %bitcast.11, s32[2,128]{1,0:T(2,128)} %bitcast.15, ...), custom_call_target="tpu_custom_call" | custom-call | tf_op jit(solution)/shard_map/pallas_call | solution.py:658
  67.3 3.0 %shard_map.129 = (f32[16,2048]{1,0:T(8,128)}, f32[16,512]{1,0:T(8,128)}, f32[512,512]{1,0:T(8,128)}, f32[512,512]{1,0:T(8,128)}, f32[4,128]{1,0:T(4,128)}) custom-call(f32[512,512]{1,0:T(8,128)} %get-tuple-element.13.rg_hbm, f32[4,128]{1,0:T(4,128)} %get-tuple-element.14.hits_hbm, bf16[2,5,16,256]{3,2,1,0:T(8,128)(2,1)} %get-tuple-element.15.f_hbm, ...), custom_call_target="tpu_custom_call" | custom-call | tf_op jit(solution)/shard_map/pallas_call | solution.py:694

commit v3 on v2

--- a/solution.py
+++ b/solution.py
@@ -20,6 +20,7 @@
 MESH = pl.DeviceIdType.MESH
 PARTS = 5
 LANES = 128
+LAG = 2
 
 
 def mm(a, b):
@@ -380,10 +381,6 @@
     def _():
         prepare()
 
-    @pl.loop(jnp.where(sec == 0, 2, 0), PARTS)
-    def _(k):
-        gradient(k, jnp.minimum(k, 1))
-
     def get_tokens(m):
         if ns > 2:
             @pl.when((sec == 1) | (sec == 3))
@@ -406,28 +403,36 @@
             token(m, 0).wait_recv()
         pack(m)
 
-    def by_section(at_zero, at_one, at_rest):
-        return jnp.where(sec == 0, at_zero, jnp.where(sec == 1, at_one, at_rest))
+    def by_section(places):
+        at = jnp.int32(places[-1])
+        for number in range(len(places) - 2, -1, -1):
+            at = jnp.where(sec == number, places[number], at)
+        return at
 
     def on_step(step, places, action):
-        start = [by_section(*place) for place in places]
+        start = [by_section(place) for place in places]
 
         @pl.when((step == start[0]) | (step == start[1]))
         def _():
             action(jnp.where(step == start[1], 1, 0))
 
-    @pl.loop(0, 11)
+    @pl.loop(jnp.where(sec == 0, 2, 0), 10)
     def _(step):
         @pl.when(step < PARTS)
         def _():
-            g1_copy(step).wait_recv()
-            total = gw_s[step, 1].astype(F32) + g1_r[step, 1].astype(F32)
-            g2_s[step] = total.astype(BF)
-            g2_copy(step).start()
-
-        @pl.when((step > 0) & (step <= PARTS))
-        def _():
-            k = step - 1
+            gradient(step, jnp.minimum(step, 1))
+
+        @pl.when((step >= LAG) & (step < PARTS + LAG))
+        def _():
+            k = step - LAG
+            g1_copy(k).wait_recv()
+            total = gw_s[k, 1].astype(F32) + g1_r[k, 1].astype(F32)
+            g2_s[k] = total.astype(BF)
+            g2_copy(k).start()
+
+        @pl.when((step > LAG) & (step <= PARTS + LAG))
+        def _():
+            k = step - LAG - 1
             g2_copy(k).wait_recv()
             total = gw_s[k, 0].astype(F32) + g1_r[k, 0].astype(F32) + g2_r[k].astype(F32)
             total = total.astype(BF)
@@ -436,16 +441,16 @@
             for d in range(1, nz):
                 gz_copy(k, d).start()
 
-        on_step(step, ((-1, 2, 5), (-1, 5, 7)), get_tokens)
+        on_step(step, ((-1, 4, 5, 6), (-1, 5, 6, 7)), get_tokens)
         on_step(
-            step, ((1, 3, 6), (2, 6, 8)),
+            step, ((2, 5, 6, 7), (4, 7, 8, 8)),
             lambda m: z_start(
                 tx_r.at[m], tz_s.at[m], tt_s.at[core, m],
                 ix_ss.at[1 + m], ix_rs.at[1 + m], iz_ss.at[1 + m], iz_rs.at[1 + m],
             ),
         )
         on_step(
-            step, ((4, 7, 9), (5, 8, 10)),
+            step, ((4, 7, 8, 8), (6, 8, 9, 9)),
             lambda m: core_start(
                 tt_s.at[core, m], iz_ss.at[1 + m], iz_rs.at[1 + m], ic_ss.at[1 + m], ic_rs.at[1 + m]
             ),

time: 70.5 us -> 66.8 us (0.948)
  the two profiles are of different devices: /device:TPU:17 before, /device:TPU:1 now
where the time goes in v3:
time: 66.8 us; the launch traced here: 66 us
  Pallas kernels  65.4 us (98%)
    pallas_call x1, Pallas kernels, exchange(): pl.pallas_call(functools.partial(kernel, dims), out_shape=(jax.ShapeDtype...  62.3 us
    pallas_call x1, Pallas kernels, local(): pl.pallas_call(functools.partial(finish, float(tokens) ** (-0.5)), out_sh...  3.02 us

profile of v3, /device:TPU:1, one launch (start us, length us, event | category | flops | bytes accessed | tf_op | source)
XLA Modules:
  0.0 66.0 jit_solution(834257581452270979)
XLA Ops:
  0.6 62.3 %shard_map.128 = (f32[512,512]{1,0:T(8,128)}, f32[4,128]{1,0:T(4,128)}, bf16[2,5,16,256]{3,2,1,0:T(8,128)(2,1)}) custom-call(bf16[2,128,512]{2,1,0:T(8,128)(2,1)} %bitcast.12, bf16[2,128,512]{2,1,0:T(8,128)(2,1)} %bitcast.13, bf16[512,2048]{1,0:T(8,128)(2,1)} %bitcast.10, bf16[512,512]{1,0:T(8,128)(2,1)} %bitcast.11, s32[2,128]{1,0:T(2,128)} %bitcast.15, ...), custom_call_target="tpu_custom_call" | custom-call | tf_op jit(solution)/shard_map/pallas_call | solution.py:663
  63.0 3.0 %shard_map.129 = (f32[16,2048]{1,0:T(8,128)}, f32[16,512]{1,0:T(8,128)}, f32[512,512]{1,0:T(8,128)}, f32[512,512]{1,0:T(8,128)}, f32[4,128]{1,0:T(4,128)}) custom-call(f32[512,512]{1,0:T(8,128)} %get-tuple-element.13.rg_hbm, f32[4,128]{1,0:T(4,128)} %get-tuple-element.14.hits_hbm, bf16[2,5,16,256]{3,2,1,0:T(8,128)(2,1)} %get-tuple-element.15.f_hbm, ...), custom_call_target="tpu_custom_call" | custom-call | tf_op jit(solution)/shard_map/pallas_call | solution.py:699

commit v4 on v3

--- a/solution.py
+++ b/solution.py
@@ -56,9 +56,9 @@
 def kernel(
     dims,
     x_hbm, og_hbm, win_hbm, wout_hbm, owner_hbm, slot_hbm,
-    rg_hbm, hits_hbm, f_hbm,
-    rg_ref, hits_ref, x_ref, win_ref, wout_ref, owner_ref, slot_ref,
-    xn_s, rx_s, act_s, slope_s, w_s, zs_s, mn_s, rm_s,
+    oh_hbm, tt_hbm, hits_hbm, f_hbm,
+    hits_ref, x_ref, win_ref, wout_ref, owner_ref, slot_ref,
+    wint_s, woutt_s, vt_s, xn_s, rx_s, act_s, slope_s, w_s, zs_s, mn_s, rm_s,
     hx_s, hx_o, lt_s, g_s, below_s, d_s, d_r,
     gw_s, g1_r, g2_s, g2_r, gz_s, gz_r, f_s,
     p_s, tk_s, idp_s, idx_r, idz_s, idt_s, tp_s, tx_r, tz_s, tt_s, oh_s,
@@ -69,10 +69,11 @@
     ns, nz, nx, cap = dims
     micro, length, width = x_ref.shape
     half = width // 2
+    mid = length // 2
     hs = width // HEADS
     scale = hs ** (-0.5)
     rows = width // (nz * nx)
-    own_rows = rg_hbm.shape[0]
+    own_rows = oh_hbm.shape[0]
     piece = length // (nz * nx)
     sec = lax.axis_index("section")
     smp = lax.axis_index("sample")
@@ -101,23 +102,22 @@
     def save(i, src, dst):
         return pltpu.make_async_copy(src, dst, out_ss.at[i])
 
-    def save_rows(b):
-        at = pl.ds(b * LANES, LANES)
-        return save(2 + b, rg_ref.at[at], rg_hbm.at[at])
-
-    loads = [
-        load(i, src, dst)
-        for i, (src, dst) in enumerate((
-            (x_hbm, x_ref), (win_hbm, win_ref), (wout_hbm, wout_ref),
-            (owner_hbm, owner_ref), (slot_hbm, slot_ref),
-        ))
-    ]
+    def save_tokens(c, m):
+        return save(3 + 2 * m + jnp.where(c == core, 0, 1), tt_s.at[c, m], tt_hbm.at[c, m])
+
+    loads = [load(0, x_hbm, x_ref)]
+    for k in range(4):
+        cols = pl.ds(k * width, width)
+        loads.append(load(1 + k, win_hbm.at[:, cols], win_ref.at[:, cols]))
+    loads.append(load(5, wout_hbm, wout_ref))
+    loads.append(load(6, owner_hbm, owner_ref))
+    loads.append(load(7, slot_hbm, slot_ref))
     for one in loads:
         one.start()
 
     @pl.when(sec == ns - 1)
     def _():
-        load(5, og_hbm, g_s).start()
+        load(8, og_hbm, g_s).start()
 
     barrier = pltpu.get_barrier_semaphore()
     peers = [other]
@@ -130,31 +130,44 @@
     row_id = lax.broadcasted_iota(jnp.int32, (length, length), 0)
     col_id = lax.broadcasted_iota(jnp.int32, (length, length), 1)
 
-    def forward(m):
-        xn, rx = normed(x_ref[m].astype(F32))
-        xn_s[m] = xn
-        rx_s[m] = rx
+    def forward():
+        all_rows = micro * length
+        loads[0].wait()
+        xn, rx = normed(x_ref[...].reshape(all_rows, width).astype(F32))
+        xn_s[...] = xn.reshape(xn_s.shape)
+        rx_s[...] = rx.reshape(rx_s.shape)
         xb = xn.astype(BF)
-        hx_s[1, m] = xb
+        hx_s[1] = xb.reshape(micro, length, width)
         for k in range(4):
-            pre = mm(xb, win_ref[:, k * width:(k + 1) * width])
+            loads[1 + k].wait()
+            block = win_ref[:, k * width:(k + 1) * width]
+            pre = mm(xb, block)
             s = sigmoid(pre)
-            act_s[m, k] = (pre * s).astype(BF)
-            slope_s[m, k] = slope(pre, s)
+            act = (pre * s).astype(BF)
+            down = slope(pre, s)
+            for m in range(micro):
+                act_s[m, k] = act[m * length:(m + 1) * length]
+                slope_s[m, k] = down[m * length:(m + 1) * length]
+            wint_s[k] = block.T
         causal = row_id >= col_id
-        mixed = []
-        for h in range(HEADS):
-            cols = slice(h * hs, (h + 1) * hs)
-            z = mm_nt(act_s[m, 2, :, cols], act_s[m, 3, :, cols]) * scale
-            s = sigmoid(z)
-            wt = jnp.where(causal, z * s, 0.0).astype(BF)
-            w_s[m, h] = wt.T
-            zs_s[m, h] = jnp.where(causal, slope(z, s), 0.0) * scale
-            mixed.append(mm(wt, act_s[m, 1, :, cols]))
-        mn, rm = normed(jnp.concatenate(mixed, -1))
-        mn_s[m] = mn
-        rm_s[m] = rm
-        hx_s[0, m] = (mn * act_s[m, 0].astype(F32)).astype(BF)
+        for m in range(micro):
+            vt_s[m] = act_s[m, 1].T
+            mixed = []
+            for h in range(HEADS):
+                cols = slice(h * hs, (h + 1) * hs)
+                z = mm_nt(act_s[m, 2, :, cols], act_s[m, 3, :, cols]) * scale
+                s = sigmoid(z)
+                wt = jnp.where(causal, z * s, 0.0).astype(BF)
+                for r in range(2):
+                    w_s[m, h, r] = wt[r * mid:(r + 1) * mid].T
+                zs_s[m, h] = jnp.where(causal, slope(z, s), 0.0) * scale
+                mixed.append(mm(wt, act_s[m, 1, :, cols]))
+            mn, rm = normed(jnp.concatenate(mixed, -1))
+            mn_s[m] = mn
+            rm_s[m] = rm
+            hx_s[0, m] = (mn * act_s[m, 0].astype(F32)).astype(BF)
+        loads[5].wait()
+        woutt_s[...] = wout_ref[...].T
 
     first = jnp.where(core == 0, 1, nx - 1)
     second = nx - first
@@ -197,42 +210,47 @@
                 gw_s[k, slot, z * rows:(z + 1) * rows, :] = part[at:at + rows]
         g1_copy(k).start()
 
-    def keep(m, k, value):
-        d_s[0, k, m] = value[:, :half]
-        d_s[1, k, m] = value[:, half:]
-        d_copy(k, m).start()
-
-    def backward(m):
-        g = g_s[m]
-        keep(m, 0, g)
-        dh = mm_nt(g, wout_ref[...])
-        mn = mn_s[m]
-        dpre = [(dh * mn * slope_s[m, 0]).astype(BF)]
-        keep(m, 1, dpre[0])
-        dmix = norm_back(dh * act_s[m, 0].astype(F32), mn, rm_s[m]).astype(BF)
+    def keep(m, k, at, value):
+        d_s[0, k, m, at] = value[:, :half]
+        d_s[1, k, m, at] = value[:, half:]
+
+    def backward(m, r, carried):
+        at = slice(r * mid, (r + 1) * mid)
+        g = g_s[m, at]
+        keep(m, 0, at, g)
+        if r == 0:
+            d_copy(0, m).start()
+        dh = mm(g, woutt_s[...])
+        mn = mn_s[m, at]
+        dpre = [(dh * mn * slope_s[m, 0, at]).astype(BF)]
+        dmix = norm_back(dh * act_s[m, 0, at].astype(F32), mn, rm_s[m, at]).astype(BF)
         dv, dq, dk = [], [], []
         for h in range(HEADS):
             cols = slice(h * hs, (h + 1) * hs)
             dm = dmix[:, cols]
-            dw = mm_nt(dm, act_s[m, 1, :, cols])
-            dv.append(mm(w_s[m, h], dm))
-            dz = (dw * zs_s[m, h]).astype(BF)
+            dw = mm(dm, vt_s[m, cols])
+            dv.append(mm(w_s[m, h, r], dm))
+            dz = (dw * zs_s[m, h, at]).astype(BF)
             dq.append(mm(dz, act_s[m, 3, :, cols]))
-            dk.append(mm(dz.T, act_s[m, 2, :, cols]))
+            dk.append(mm(dz.T, act_s[m, 2, at, cols]))
+        dv, dq, dk = (jnp.concatenate(part, -1) for part in (dv, dq, dk))
+        if r == 1:
+            carried = (dv[:mid], dk[:mid])
+            dv, dk = dv[mid:], dk[mid:]
+        else:
+            dv, dk = dv[:mid] + carried[0], dk[:mid] + carried[1]
         for k, part in enumerate((dv, dq, dk)):
-            dpre.append((jnp.concatenate(part, -1) * slope_s[m, k + 1]).astype(BF))
-            keep(m, k + 2, dpre[-1])
-
-        @pl.when((sec == 0) & (m == micro - 1))
-        def _():
-            gradient(0, 0)
-            gradient(1, 1)
-
-        dxn = mm_nt(dpre[0], win_ref[:, :width])
+            dpre.append((part * slope_s[m, k + 1, at]).astype(BF))
+        for k in range(4):
+            keep(m, k + 1, at, dpre[k])
+            if r == 0:
+                d_copy(k + 1, m).start()
+        dxn = mm(dpre[0], wint_s[0])
         for k in range(1, 4):
-            dxn = dxn + mm_nt(dpre[k], win_ref[:, k * width:(k + 1) * width])
-        below = norm_back(dxn, xn_s[m], rx_s[m]) + g.astype(F32)
-        below_s[m] = below.astype(BF)
+            dxn = dxn + mm(dpre[k], wint_s[k])
+        below = norm_back(dxn, xn_s[m, at], rx_s[m, at]) + g.astype(F32)
+        below_s[m, at] = below.astype(BF)
+        return carried
 
     def pack_plan(m):
         owner = owner_ref[m:m + 1, :]
@@ -275,18 +293,28 @@
             remote(mine.at[d], mine.at[d], zs.at[d], zr.at[d], z_peer(d)).wait_recv()
         remote(mine, mine, ss, rs, other).start()
 
-    def prepare():
-        remote(hx_s, hx_o, hx_ss.at[0], hx_rs.at[0], other).start()
+    def prepare_own():
         ids = jnp.concatenate([pack_plan(m) for m in range(micro)], -1)
         idp_s[...] = ids.reshape(idp_s.shape)
-        x_start(idp_s, idx_r, ix_ss.at[0], ix_rs.at[0])
         for kind in range(2):
             lt_s[kind, 0] = hx_s[kind].reshape(micro * length, width).T
+
+    def prepare_sends():
+        remote(hx_s, hx_o, hx_ss.at[0], hx_rs.at[0], other).start()
+        x_start(idp_s, idx_r, ix_ss.at[0], ix_rs.at[0])
+
+    def ids_along_z():
         z_start(idx_r, idz_s, idt_s.at[core], ix_ss.at[0], ix_rs.at[0], iz_ss.at[0], iz_rs.at[0])
+
+    def prepare_other():
         remote(hx_s, hx_o, hx_ss.at[0], hx_rs.at[0], other).wait_recv()
         for kind in range(2):
             lt_s[kind, 1] = hx_o[kind].reshape(micro * length, width).T
+
+    def ids_over():
         core_start(idt_s.at[core], iz_ss.at[0], iz_rs.at[0], ic_ss.at[0], ic_rs.at[0])
+
+    def ids_done():
         remote(idt_s.at[1 - core], idt_s.at[1 - core], ic_ss.at[0], ic_rs.at[0], other).wait_recv()
         hits = jnp.zeros((own_rows, 1), F32)
         own_id = lax.broadcasted_iota(jnp.int32, (own_rows, length), 0).astype(F32)
@@ -301,52 +329,46 @@
             column = hits[b * LANES:(b + 1) * LANES]
             hits_ref[b:b + 1, :] = jnp.broadcast_to(column, (LANES, LANES)).T[:1]
         save(0, hits_ref, hits_hbm).start()
-
-    loads[0].wait()
-    loads[1].wait()
+        save(2, oh_s, oh_hbm).start()
+
+    forward()
+    for one in loads[6:]:
+        one.wait()
+
+    @pl.when(sec == ns - 1)
+    def _():
+        load(8, og_hbm, g_s).wait()
+
+    pl.semaphore_wait(barrier, len(peers))
+
+    early = ns // 2
 
     @pl.when(sec < ns - 1)
     def _():
-        @pl.loop(0, micro)
-        def _(m):
-            forward(m)
-
-    @pl.when(sec == ns - 1)
-    def _():
-        forward(0)
-
-    for one in loads[2:]:
-        one.wait()
-
-    @pl.when(sec == ns - 1)
-    def _():
-        load(5, og_hbm, g_s).wait()
-
-    pl.semaphore_wait(barrier, len(peers))
-
-    early = ns // 2
+        prepare_own()
+        prepare_sends()
 
     @pl.when(sec < early)
     def _():
-        prepare()
-
-    def hop(m):
+        ids_along_z()
+        prepare_other()
+        ids_over()
+        ids_done()
+
+    def hop(m, r):
+        at = pl.ds(r * mid, mid)
         return remote(
-            below_s.at[m], g_s.at[m], hop_ss.at[m], hop_rs.at[m],
+            below_s.at[m, at], g_s.at[m, at], hop_ss.at[m, r], hop_rs.at[m, r],
             (wrap(sec + ns - 1, ns), smp, core),
         )
 
-    def token(m, place):
+    def token(m, r, to):
+        at = pl.ds(r * mid, mid)
         return remote(
-            below_s.at[m], tk_s.at[m], tk_ss.at[m, place], tk_rs.at[m, 0],
-            (1 if place == 0 else ns - 1, smp, core),
+            below_s.at[m, at], tk_s.at[m, at], tk_ss.at[m, r, to], tk_rs.at[m, r], (to, smp, core)
         )
 
-    def token_on(m, place):
-        span = pl.ds(place * (length // 2), length // 2)
-        return remote(
-            tk_s.at[m, span], tk_s.at[m, span], tk_ss.at[m, 0], tk_rs.at[m, place], (2, smp, core)
-        )
+    far_first = sorted(range(1, ns), key=lambda to: -min(to, ns - to))
 
     def pack(m):
         packed = mm(p_s[m], tk_s[m]).astype(BF)
@@ -355,52 +377,40 @@
 
     @pl.loop(0, micro)
     def _(m):
-        @pl.when((sec == ns - 1) & (m > 0))
-        def _():
-            forward(m)
-
-        @pl.when(sec < ns - 1)
-        def _():
-            hop(m).wait_recv()
-
-        backward(m)
-
-        @pl.when(sec > 0)
-        def _():
-            hop(m).start()
+        carried = None
+        for r in (1, 0):
+            @pl.when(sec < ns - 1)
+            def _():
+                hop(m, r).wait_recv()
+
+            carried = backward(m, r, carried)
+
+            @pl.when(sec > 0)
+            def _():
+                hop(m, r).start()
+
+            @pl.when(sec == 0)
+            def _():
+                for to in far_first:
+                    token(m, r, to).start()
 
         @pl.when(sec == 0)
         def _():
             tk_s[m] = below_s[m]
-            token(m, 0).start()
-            if ns > 2:
-                token(m, 1).start()
             pack(m)
+
+    @pl.when(sec == ns - 1)
+    def _():
+        prepare_own()
+        prepare_sends()
 
     @pl.when(sec >= early)
     def _():
-        prepare()
+        prepare_other()
 
     def get_tokens(m):
-        if ns > 2:
-            @pl.when((sec == 1) | (sec == 3))
-            def _():
-                token(m, 0).wait_recv()
-
-            @pl.when(sec == 1)
-            def _():
-                token_on(m, 0).start()
-
-            @pl.when(sec == 3)
-            def _():
-                token_on(m, 1).start()
-
-            @pl.when(sec == 2)
-            def _():
-                token_on(m, 0).wait_recv()
-                token_on(m, 1).wait_recv()
-        else:
-            token(m, 0).wait_recv()
+        for r in range(2):
+            token(m, r, 1).wait_recv()
         pack(m)
 
     def by_section(places):
@@ -416,7 +426,11 @@
         def _():
             action(jnp.where(step == start[1], 1, 0))
 
-    @pl.loop(jnp.where(sec == 0, 2, 0), 10)
+    def send_over(m):
+        core_start(tt_s.at[core, m], iz_ss.at[1 + m], iz_rs.at[1 + m], ic_ss.at[1 + m], ic_rs.at[1 + m])
+        save_tokens(core, m).start()
+
+    @pl.loop(0, 10)
     def _(step):
         @pl.when(step < PARTS)
         def _():
@@ -441,9 +455,14 @@
             for d in range(1, nz):
                 gz_copy(k, d).start()
 
+        for place, action in ((1, ids_along_z), (3, ids_over), (5, ids_done)):
+            @pl.when((step == place) & (sec >= early))
+            def _():
+                action()
+
         on_step(step, ((-1, 4, 5, 6), (-1, 5, 6, 7)), get_tokens)
         on_step(
-            step, ((2, 5, 6, 7), (4, 7, 8, 8)),
+            step, ((2, 5, 6, 7), (4, 7, 7, 8)),
             lambda m: z_start(
                 tx_r.at[m], tz_s.at[m], tt_s.at[core, m],
                 ix_ss.at[1 + m], ix_rs.at[1 + m], iz_ss.at[1 + m], iz_rs.at[1 + m],
@@ -451,9 +470,7 @@
         )
         on_step(
             step, ((4, 7, 8, 8), (6, 8, 9, 9)),
-            lambda m: core_start(
-                tt_s.at[core, m], iz_ss.at[1 + m], iz_rs.at[1 + m], ic_ss.at[1 + m], ic_rs.at[1 + m]
-            ),
+            send_over,
         )
 
     total = gz_s[zz].astype(F32)
@@ -468,11 +485,7 @@
         remote(
             tt_s.at[1 - core, m], tt_s.at[1 - core, m], ic_ss.at[1 + m], ic_rs.at[1 + m], other
         ).wait_recv()
-    tokens = tt_s[...].reshape(2 * micro * length, width)
-    for b in range(own_rows // LANES):
-        at = slice(b * LANES, (b + 1) * LANES)
-        rg_ref[at, :] = mm(oh_s[at, :], tokens)
-        save_rows(b).start()
+        save_tokens(1 - core, m).start()
     remote(f_s.at[1 - core], f_s.at[1 - core], f_ss.at[0], f_rs.at[0], other).wait_recv()
     save(1, f_s, f_hbm).start()
 
@@ -502,65 +515,61 @@
                 outbox.at[wrap(zz + d, nz)], full.at[d], iz_ss.at[i, d], iz_rs.at[i, d], z_peer(d)
             ).wait_send()
         remote(full, full, ic_ss.at[i], ic_rs.at[i], other).wait_send()
+    @pl.when(sec > 0)
+    def _():
+        for m in range(micro):
+            for r in range(2):
+                hop(m, r).wait_send()
+
     for m in range(micro):
-        @pl.when(sec > 0)
-        def _():
-            hop(m).wait_send()
-
         @pl.when(sec == 0)
         def _():
-            token(m, 0).wait_send()
-            if ns > 2:
-                token(m, 1).wait_send()
-
-        if ns > 2:
-            @pl.when(sec == 1)
-            def _():
-                token_on(m, 0).wait_send()
-
-            @pl.when(sec == 3)
-            def _():
-                token_on(m, 1).wait_send()
+            for to in range(1, ns):
+                for r in range(2):
+                    token(m, r, to).wait_send()
 
     save(0, hits_ref, hits_hbm).wait()
     save(1, f_s, f_hbm).wait()
-    for b in range(own_rows // LANES):
-        save_rows(b).wait()
+    save(2, oh_s, oh_hbm).wait()
+    for m in range(micro):
+        for c in (core, 1 - core):
+            save_tokens(c, m).wait()
 
 
 def finish(
     factor,
-    rg_hbm, hits_hbm, f_hbm, table_in, moment_in, second_in,
+    oh_hbm, tt_hbm, hits_hbm, f_hbm, table_in, moment_in, second_in,
     gi_hbm, go_hbm, table_hbm, moment_hbm, second_hbm,
-    rg_ref, hits_ref, f_ref, table_ref, moment_ref, second_ref, gi_s, go_s, table_s, moment_s, second_s, in_sems, sems,
+    oh_ref, tt_ref, hits_ref, f_ref, table_ref, moment_ref, second_ref, gi_s, go_s, table_s, moment_s, second_s, in_sems, sems,
 ):
     half = f_ref.shape[-1]
     width = 2 * half
-    blocks = rg_ref.shape[0] // LANES
+    blocks = oh_ref.shape[0] // LANES
 
     copies = []
 
     loads = [
         pltpu.make_async_copy(src, dst, in_sems.at[i])
-        for i, (src, dst) in enumerate(((hits_hbm, hits_ref), (second_in, second_ref), (f_hbm, f_ref)))
+        for i, (src, dst) in enumerate(((tt_hbm, tt_ref), (hits_hbm, hits_ref), (second_in, second_ref), (f_hbm, f_ref)))
     ]
 
     def row_loads(b):
         at = pl.ds(b * LANES, LANES)
-        pairs = ((rg_hbm, rg_ref), (moment_in, moment_ref), (table_in, table_ref))
+        pairs = ((oh_hbm, oh_ref), (moment_in, moment_ref), (table_in, table_ref))
         return [
-            pltpu.make_async_copy(src.at[at], dst.at[at], in_sems.at[3 + 3 * b + i])
+            pltpu.make_async_copy(src.at[at], dst.at[at], in_sems.at[4 + 3 * b + i])
             for i, (src, dst) in enumerate(pairs)
         ]
 
-    loads[0].start()
-    loads[1].start()
+    for load in loads[:3]:
+        load.start()
     for b in range(blocks):
         for load in row_loads(b):
             load.start()
-    loads[2].start()
-    loads[0].wait()
-    loads[1].wait()
+    loads[3].start()
+    for load in loads[:3]:
+        load.wait()
+    tokens = tt_ref[...].reshape(oh_ref.shape[1], width)
 
     def put(src, dst):
         copy = pltpu.make_async_copy(src, dst, sems.at[len(copies)])
@@ -571,7 +580,7 @@
         at = pl.ds(b * LANES, LANES)
         for load in row_loads(b):
             load.wait()
-        grad = rg_ref[at, :]
+        grad = mm(oh_ref[at, :], tokens)
         hit = jnp.broadcast_to(hits_ref[b:b + 1, :], (LANES, LANES)).T > 0.5
         wide = jnp.concatenate([hit] * (width // LANES), -1)
         square = jnp.mean(grad * grad, -1, keepdims=True)
@@ -588,7 +597,7 @@
         table_s[at, :] = jnp.where(wide, old_table - STEP_SIZE * moment / below, old_table)
         put(table_s.at[at], table_hbm.at[at])
     put(second_s, second_hbm)
-    loads[2].wait()
+    loads[3].wait()
     for c in range(2):
         go_s[:, c * half:(c + 1) * half] = f_ref[c, 0].astype(F32) * factor
         for k in range(4):
@@ -611,18 +620,20 @@
     streams = 1 + micro
     wide = LANES * micro
     scratch = [
-        vm((own_rows, width), F32),
         vm((own_rows // LANES, LANES), F32),
         vm((micro, length, width), BF),
         vm((width, 4 * width), BF),
         vm((width, width), BF),
         vm((micro, length), jnp.int32),
         vm((micro, length), jnp.int32),
+        vm((4, width, width), BF),
+        vm((width, width), BF),
+        vm((micro, width, length), BF),
         vm((micro, length, width), F32),
         vm((micro, length, 1), F32),
         vm((micro, 4, length, width), BF),
         vm((micro, 4, length, width), F32),
-        vm((micro, HEADS, length, length), BF),
+        vm((micro, HEADS, 2, length, length // 2), BF),
         vm((micro, HEADS, length, length), F32),
         vm((micro, length, width), F32),
         vm((micro, length, 1), F32),
@@ -651,11 +662,11 @@
         vm((micro, nz, lz, width), BF),
         vm((2, micro, nz, lz, width), BF),
         vm((own_rows, 2 * micro * length), BF),
-        dma((6,)), dma((2 + own_rows // LANES,)), dma((micro,)), dma((micro,)), dma((1,)), dma((1,)),
+        dma((9,)), dma((3 + 2 * micro,)), dma((micro, 2)), dma((micro, 2)), dma((1,)), dma((1,)),
         dma((PARTS, micro)), dma((PARTS, micro)),
         dma((PARTS,)), dma((PARTS,)), dma((PARTS,)), dma((PARTS,)),
         dma((nz, PARTS)), dma((nz, PARTS)), dma((1,)), dma((1,)),
-        dma((micro, 2)), dma((micro, 2)),
+        dma((micro, 2, 4)), dma((micro, 2)),
         dma((streams, nx)), dma((streams, nx)),
         dma((streams, nz)), dma((streams, nz)),
         dma((streams,)), dma((streams,)),
@@ -663,12 +674,13 @@
     return pl.pallas_call(
         functools.partial(kernel, dims),
         out_shape=(
-            jax.ShapeDtypeStruct((own_rows, width), F32),
+            jax.ShapeDtypeStruct((own_rows, 2 * micro * length), BF),
+            jax.ShapeDtypeStruct((2, micro, nz, lz, width), BF),
             jax.ShapeDtypeStruct((own_rows // LANES, LANES), F32),
             jax.ShapeDtypeStruct((2, PARTS, rows, half), BF),
         ),
         in_specs=[pl.BlockSpec(memory_space=pltpu.HBM)] * 6,
-        out_specs=[pl.BlockSpec(memory_space=pltpu.HBM)] * 3,
+        out_specs=[pl.BlockSpec(memory_space=pltpu.HBM)] * 4,
         scratch_shapes=scratch,
         compiler_params=pltpu.CompilerParams(
             collective_id=0, has_side_effects=True, vmem_limit_bytes=56 << 20
@@ -683,7 +695,7 @@
     cap = max(2, 2 * BLOCK // owners)
     own_rows = table.shape[0]
     rows = width // (nz * nx)
-    row_grad, hits, grads = exchange(
+    hot, tokens_in, hits, grads = exchange(
         (ns, nz, nx, cap),
         saved_input[0, :, 0],
         out_grad[:, 0],
@@ -699,14 +711,14 @@
     grad_in, grad_out, table_new, moment_new, second_new = pl.pallas_call(
         functools.partial(finish, float(tokens) ** (-0.5)),
         out_shape=[jax.ShapeDtypeStruct(shape, F32) for shape in shapes],
-        in_specs=[pl.BlockSpec(memory_space=pltpu.HBM)] * 6,
+        in_specs=[pl.BlockSpec(memory_space=pltpu.HBM)] * 7,
         out_specs=[pl.BlockSpec(memory_space=pltpu.HBM)] * 5,
-        scratch_shapes=[pltpu.VMEM(part.shape, part.dtype) for part in (row_grad, hits, grads)]
+        scratch_shapes=[pltpu.VMEM(part.shape, part.dtype) for part in (hot, tokens_in, hits, grads)]
         + [pltpu.VMEM(shape, F32) for shape in shapes[2:]]
         + [pltpu.VMEM(shape, F32) for shape in shapes]
-        + [pltpu.SemaphoreType.DMA((3 + 3 * lines[0],)), pltpu.SemaphoreType.DMA((2 * lines[0] + 3,))],
+        + [pltpu.SemaphoreType.DMA((4 + 3 * lines[0],)), pltpu.SemaphoreType.DMA((2 * lines[0] + 3,))],
         compiler_params=pltpu.CompilerParams(vmem_limit_bytes=56 << 20),
-    )(row_grad, hits, grads, table, moment, second.reshape(lines))
+    )(hot, tokens_in, hits, grads, table, moment, second.reshape(lines))
     return (grad_in[None], grad_out[None], table_new, moment_new, second_new.reshape(own_rows))
 
 

time: 66.8 us -> 65.5 us (0.981); the launches traced: 66 us -> 65.4 us
    pallas_call x1, Pallas kernels: 62.3 us -> 61 us  [exchange(): pl.pallas_call(functools.partial(kernel, dims), out_shape=(jax.ShapeDtype...]
    pallas_call x1, Pallas kernels: 3.02 us -> 3.77 us  [local(): pl.pallas_call(functools.partial(finish, float(tokens) ** (-0.5)), out_sh...]
where the time goes in v4:
time: 65.5 us; the launch traced here: 65.4 us
  Pallas kernels  64.8 us (99%)
    pallas_call x1, Pallas kernels, exchange(): pl.pallas_call(functools.partial(kernel, dims), out_shape=(jax.ShapeDtype...  61 us
    pallas_call x1, Pallas kernels, local(): pl.pallas_call(functools.partial(finish, float(tokens) ** (-0.5)), out_sh...  3.77 us

profile of v4, /device:TPU:1, one launch (start us, length us, event | category | flops | bytes accessed | tf_op | source)
XLA Modules:
  0.0 65.4 jit_solution(12153678820289783478)
XLA Ops:
  0.6 61.0 %shard_map.128 = (bf16[512,512]{1,0:T(8,128)(2,1)}, bf16[2,2,8,16,512]{4,3,2,1,0:T(8,128)(2,1)}, f32[4,128]{1,0:T(4,128)}, bf16[2,5,16,256]{3,2,1,0:T(8,128)(2,1)}) custom-call(bf16[2,128,512]{2,1,0:T(8,128)(2,1)} %bitcast.12, bf16[2,128,512]{2,1,0:T(8,128)(2,1)} %bitcast.13, bf16[512,2048]{1,0:T(8,128)(2,1)} %bitcast.10, bf16[512,512]{1,0:T(8,128)(2,1)} %bitcast.11, ...), custom_call_target="tpu_custom_call" | custom-call | tf_op jit(solution)/shard_map/pallas_call | solution.py:674
  61.6 3.8 %shard_map.129 = (f32[16,2048]{1,0:T(8,128)}, f32[16,512]{1,0:T(8,128)}, f32[512,512]{1,0:T(8,128)}, f32[512,512]{1,0:T(8,128)}, f32[4,128]{1,0:T(4,128)}) custom-call(bf16[512,512]{1,0:T(8,128)(2,1)} %get-tuple-element.14.oh_hbm, bf16[2,2,8,16,512]{4,3,2,1,0:T(8,128)(2,1)} %get-tuple-element.15.tt_hbm, f32[4,128]{1,0:T(4,128)} %get-tuple-element.16.hits_hbm, ...), custom_call_target="tpu_custom_call" | custom-call | tf_op jit(solution)/shard_map/pallas_call | solution.py:711

commit v5 on v4

--- a/solution.py
+++ b/solution.py
@@ -85,6 +85,8 @@
 
     def x_peer(d):
         return (sec, zz * nx + wrap(xx + d, nx), core)
+
+    z_order = sorted(range(1, nz), key=lambda d: -min(d, nz - d))
 
     def z_peer(d):
         return (sec, wrap(zz + d, nz) * nx + xx, core)
@@ -285,7 +287,7 @@
         moved = mm(turn, stacked).astype(BF)
         outbox[...] = moved.reshape(outbox.shape)
         total[0] = outbox[zz]
-        for d in range(1, nz):
+        for d in z_order:
             remote(outbox.at[wrap(zz + d, nz)], total.at[d], ss.at[d], rs.at[d], z_peer(d)).start()
 
     def core_start(mine, zs, zr, ss, rs):
@@ -397,7 +399,10 @@
         @pl.when(sec == 0)
         def _():
             tk_s[m] = below_s[m]
-            pack(m)
+
+            @pl.when(m < micro - 1)
+            def _():
+                pack(m)
 
     @pl.when(sec == ns - 1)
     def _():
@@ -409,8 +414,11 @@
         prepare_other()
 
     def get_tokens(m):
-        for r in range(2):
-            token(m, r, 1).wait_recv()
+        @pl.when(sec > 0)
+        def _():
+            for r in range(2):
+                token(m, r, 1).wait_recv()
+
         pack(m)
 
     def by_section(places):
@@ -452,7 +460,7 @@
             total = total.astype(BF)
             for z in range(nz):
                 gz_s[z, k] = total[z * rows:(z + 1) * rows]
-            for d in range(1, nz):
+            for d in z_order:
                 gz_copy(k, d).start()
 
         for place, action in ((1, ids_along_z), (3, ids_over), (5, ids_done)):
@@ -460,7 +468,7 @@
             def _():
                 action()
 
-        on_step(step, ((-1, 4, 5, 6), (-1, 5, 6, 7)), get_tokens)
+        on_step(step, ((-1, 4, 5, 6), (1, 5, 6, 7)), get_tokens)
         on_step(
             step, ((2, 5, 6, 7), (4, 7, 7, 8)),
             lambda m: z_start(
@@ -469,7 +477,7 @@
             ),
         )
         on_step(
-            step, ((4, 7, 8, 8), (6, 8, 9, 9)),
+            step, ((6, 7, 8, 8), (8, 8, 9, 9)),
             send_over,
         )
 

time: 65.5 us -> 65.1 us (level)
  no operation moved by 1% of the time
where the time goes in v5:
time: 65.1 us; the launch traced here: 65 us
  Pallas kernels  64.4 us (99%)
    pallas_call x1, Pallas kernels, exchange(): pl.pallas_call(functools.partial(kernel, dims), out_shape=(jax.ShapeDtype...  60.6 us
    pallas_call x1, Pallas kernels, local(): pl.pallas_call(functools.partial(finish, float(tokens) ** (-0.5)), out_sh...  3.77 us

profile of v5, /device:TPU:1, one launch (start us, length us, event | category | flops | bytes accessed | tf_op | source)
XLA Modules:
  0.0 65.0 jit_solution(15542469264609383584)
XLA Ops:
  0.6 60.6 %shard_map.128 = (bf16[512,512]{1,0:T(8,128)(2,1)}, bf16[2,2,8,16,512]{4,3,2,1,0:T(8,128)(2,1)}, f32[4,128]{1,0:T(4,128)}, bf16[2,5,16,256]{3,2,1,0:T(8,128)(2,1)}) custom-call(bf16[2,128,512]{2,1,0:T(8,128)(2,1)} %bitcast.12, bf16[2,128,512]{2,1,0:T(8,128)(2,1)} %bitcast.13, bf16[512,2048]{1,0:T(8,128)(2,1)} %bitcast.10, bf16[512,512]{1,0:T(8,128)(2,1)} %bitcast.11, ...), custom_call_target="tpu_custom_call" | custom-call | tf_op jit(solution)/shard_map/pallas_call | solution.py:682
  61.3 3.8 %shard_map.129 = (f32[16,2048]{1,0:T(8,128)}, f32[16,512]{1,0:T(8,128)}, f32[512,512]{1,0:T(8,128)}, f32[512,512]{1,0:T(8,128)}, f32[4,128]{1,0:T(4,128)}) custom-call(bf16[512,512]{1,0:T(8,128)(2,1)} %get-tuple-element.14.oh_hbm, bf16[2,2,8,16,512]{4,3,2,1,0:T(8,128)(2,1)} %get-tuple-element.15.tt_hbm, f32[4,128]{1,0:T(4,128)} %get-tuple-element.16.hits_hbm, ...), custom_call_target="tpu_custom_call" | custom-call | tf_op jit(solution)/shard_map/pallas_call | solution.py:719

commit v6 on v5

--- a/solution.py
+++ b/solution.py
@@ -20,7 +20,7 @@
 MESH = pl.DeviceIdType.MESH
 PARTS = 5
 LANES = 128
-LAG = 2
+LAG = 3
 
 
 def mm(a, b):

time: 65.1 us -> 65.1 us (level)
  no operation moved by 1% of the time
where the time goes in v6:
time: 65.1 us; the launch traced here: 65 us
  Pallas kernels  64.4 us (99%)
    pallas_call x1, Pallas kernels, exchange(): pl.pallas_call(functools.partial(kernel, dims), out_shape=(jax.ShapeDtype...  60.6 us
    pallas_call x1, Pallas kernels, local(): pl.pallas_call(functools.partial(finish, float(tokens) ** (-0.5)), out_sh...  3.77 us

profile of v6, /device:TPU:1, one launch (start us, length us, event | category | flops | bytes accessed | tf_op | source)
XLA Modules:
  0.0 65.0 jit_solution(6158125892986656537)
XLA Ops:
  0.6 60.6 %shard_map.128 = (bf16[512,512]{1,0:T(8,128)(2,1)}, bf16[2,2,8,16,512]{4,3,2,1,0:T(8,128)(2,1)}, f32[4,128]{1,0:T(4,128)}, bf16[2,5,16,256]{3,2,1,0:T(8,128)(2,1)}) custom-call(bf16[2,128,512]{2,1,0:T(8,128)(2,1)} %bitcast.12, bf16[2,128,512]{2,1,0:T(8,128)(2,1)} %bitcast.13, bf16[512,2048]{1,0:T(8,128)(2,1)} %bitcast.10, bf16[512,512]{1,0:T(8,128)(2,1)} %bitcast.11, ...), custom_call_target="tpu_custom_call" | custom-call | tf_op jit(solution)/shard_map/pallas_call | solution.py:682
  61.3 3.8 %shard_map.129 = (f32[16,2048]{1,0:T(8,128)}, f32[16,512]{1,0:T(8,128)}, f32[512,512]{1,0:T(8,128)}, f32[512,512]{1,0:T(8,128)}, f32[4,128]{1,0:T(4,128)}) custom-call(bf16[512,512]{1,0:T(8,128)(2,1)} %get-tuple-element.14.oh_hbm, bf16[2,2,8,16,512]{4,3,2,1,0:T(8,128)(2,1)} %get-tuple-element.15.tt_hbm, f32[4,128]{1,0:T(4,128)} %get-tuple-element.16.hits_hbm, ...), custom_call_target="tpu_custom_call" | custom-call | tf_op jit(solution)/shard_map/pallas_call | solution.py:719
